TPU v7x, 32 devices: a whole 2x2x4 slice. The times are simulated.
32 devices in a mesh: fsdp: 8 (over z, core), rep: 2 (over y), cp: 2 (over x).
Axes of the slice: x: 2, y: 2, z: 4, core: 2. Of those that a mesh axis runs over, the one named last changes fastest.
Arguments:
- block_input: bfloat16 [16, 768, 576], P(('fsdp', 'rep'), 'cp'), may hold values from -6 to 6
- segment_ids: int32 [16, 768], P(('fsdp', 'rep'), 'cp'), may hold values from 0 to 3, as said below
- attn_gain: bfloat16 [576], P('fsdp'), may hold values from 0.5 to 1.5
- w_qkv: bfloat16 [576, 960], P('fsdp'), as said below
- w_out: bfloat16 [576, 576], P('fsdp'), may hold values from -0.75 to 0.75
- mlp_gain: bfloat16 [576], P('fsdp'), may hold values from 0.5 to 1.5
- w_gate: bfloat16 [576, 1536], P('fsdp'), may hold values from -0.25 to 0.25
- w_up: bfloat16 [576, 1536], P('fsdp'), may hold values from -0.25 to 0.25
- w_down: bfloat16 [1536, 576], P('fsdp'), may hold values from -0.15625 to 0.15625
- out_cotangent: bfloat16 [16, 768, 576], P(('fsdp', 'rep'), 'cp'), may hold values from -6 to 6
Outputs:
- block_output: bfloat16 [16, 768, 576], P(('fsdp', 'rep'), 'cp')
- input_grad: float32 [16, 768, 576], P(('fsdp', 'rep'), 'cp')
- attn_gain_grad: float32 [576], P('fsdp')
- qkv_grad: float32 [576, 960], P('fsdp')
- out_grad: float32 [576, 576], P('fsdp')
- mlp_gain_grad: float32 [576], P('fsdp')
- gate_grad: float32 [576, 1536], P('fsdp')
- up_grad: float32 [576, 1536], P('fsdp')
- down_grad: float32 [1536, 576], P('fsdp')
Inputs may be any that keep to these rules, and one draw needn't show every extreme that they name: `segment_ids`: along each sequence the numbers start at 0 and rise by one at each document boundary; every sequence holds 4 documents, each of 48 to 384 tokens, and exactly one of them has 384 tokens. `w_qkv`: independent entries.
All inputs are finite; a program needn't handle non-finite values.
Results may differ from a plain program's by a relative error of at most 0.011.
Values may be sent and summed in bfloat16 or wider, within the bound.
A program may use at most 128 MiB of HBM per device.

v0:
```python
import jax
import jax.numpy as jnp
from jax import lax
from jax.sharding import PartitionSpec as P

QUERY_HEADS = 9
KEY_VALUE_HEADS = 3
HEAD_SIZE = 64


EPS = 1e-05
THETA = 100000.0
MASKED = -1e30


def rope_tables(positions):
    half = HEAD_SIZE // 2
    freq = THETA ** (-2.0 * jnp.arange(half, dtype=jnp.float32) / HEAD_SIZE)
    angle = positions.astype(jnp.float32)[:, None] * freq[None, :]
    return (jnp.cos(angle), jnp.sin(angle))


def apply_rotation(tensor, cosine_table, sine_table, direction):
    half = HEAD_SIZE // 2
    first = tensor[..., :half]
    second = tensor[..., half:]
    cos_b = cosine_table[:, None, :]
    sin_b = sine_table[:, None, :] * direction
    return jnp.concatenate(
        [first * cos_b - second * sin_b, first * sin_b + second * cos_b], axis=-1
    )


def doc_positions(seg_row):
    index_row = jnp.arange(seg_row.shape[0], dtype=jnp.int32)
    starts = jnp.sum((seg_row[None, :] < seg_row[:, None]).astype(jnp.int32), axis=1)
    return index_row - starts


def times_transposed(left, right):
    return lax.dot_general(
        left, right, (((1,), (1,)), ((), ())), preferred_element_type=jnp.float32
    )


def transposed_times(left, right):
    return lax.dot_general(
        left, right, (((0,), (0,)), ((), ())), preferred_element_type=jnp.float32
    )


def norm_forward(values, gain):
    inv_rms = lax.rsqrt(jnp.mean(values * values, axis=-1, keepdims=True) + EPS)
    normed = values * inv_rms
    return (normed, inv_rms, (normed * gain.astype(jnp.float32)).astype(jnp.bfloat16))


def norm_backward(d_normed, normed, inv_rms, gain):
    gain_grad = jnp.sum(d_normed * normed, axis=0)
    scaled = d_normed * gain.astype(jnp.float32)
    return (
        gain_grad,
        inv_rms * (scaled - normed * jnp.mean(scaled * normed, axis=-1, keepdims=True)),
    )


def score_block(query_rows, keys_three_axis, visible):
    row_span = query_rows.shape[0]
    grouped_heads = query_rows.reshape(
        row_span, KEY_VALUE_HEADS, QUERY_HEADS // KEY_VALUE_HEADS, HEAD_SIZE
    )
    scores = jnp.einsum(
        "nkgd,mkd->kgnm", grouped_heads, keys_three_axis, preferred_element_type=jnp.float32
    ) * HEAD_SIZE ** (-0.5)
    return jnp.where(visible[None, None], scores, MASKED)


def attend(query_rows, keys_three_axis, values_three_axis, visible):
    row_span = query_rows.shape[0]
    scores = score_block(query_rows, keys_three_axis, visible)
    top = jnp.max(scores, axis=-1, keepdims=True)
    expo = jnp.exp(scores - top)
    total = jnp.sum(expo, axis=-1, keepdims=True)
    probs = (expo / total).astype(jnp.bfloat16)
    log_total = top + jnp.log(total)
    mixed_heads = jnp.einsum(
        "kgnm,mkd->nkgd", probs, values_three_axis, preferred_element_type=jnp.float32
    )
    return (mixed_heads.reshape(row_span, QUERY_HEADS * HEAD_SIZE).astype(jnp.bfloat16), log_total)


def attend_back(
    mixed_gradient, mixed_heads, query_rows, keys_three_axis, values_three_axis, visible, log_total
):
    row_span = query_rows.shape[0]
    query_group = QUERY_HEADS // KEY_VALUE_HEADS
    scores = score_block(query_rows, keys_three_axis, visible)
    probs = jnp.exp(scores - log_total)
    probs_b = probs.astype(jnp.bfloat16)
    grouped_gradient = mixed_gradient.reshape(row_span, KEY_VALUE_HEADS, query_group, HEAD_SIZE)
    d_values = jnp.einsum(
        "kgnm,nkgd->mkd", probs_b, grouped_gradient, preferred_element_type=jnp.float32
    )
    d_probs = jnp.einsum(
        "nkgd,mkd->kgnm", grouped_gradient, values_three_axis, preferred_element_type=jnp.float32
    )
    change_amount = jnp.sum(
        grouped_gradient.astype(jnp.float32)
        * mixed_heads.reshape(row_span, KEY_VALUE_HEADS, query_group, HEAD_SIZE).astype(
            jnp.float32
        ),
        axis=-1,
    )
    change_amount = jnp.transpose(change_amount, (1, 2, 0))[..., None]
    d_scores = (probs * (d_probs - change_amount)).astype(jnp.bfloat16)
    grouped_heads = query_rows.reshape(row_span, KEY_VALUE_HEADS, query_group, HEAD_SIZE)
    d_queries = jnp.einsum(
        "kgnm,mkd->nkgd", d_scores, keys_three_axis, preferred_element_type=jnp.float32
    ) * HEAD_SIZE ** (-0.5)
    d_keys = jnp.einsum(
        "kgnm,nkgd->mkd", d_scores, grouped_heads, preferred_element_type=jnp.float32
    ) * HEAD_SIZE ** (-0.5)
    return (d_queries.reshape(row_span, QUERY_HEADS, HEAD_SIZE), d_keys, d_values)


def shards(
    block_input, segment_ids, attn_gain, w_qkv, w_out, mlp_gain, w_gate, w_up, w_down, out_cotangent
):
    residual = block_input[0].astype(jnp.float32)
    row_span = residual.shape[0]
    query_columns = QUERY_HEADS * HEAD_SIZE
    key_columns = KEY_VALUE_HEADS * HEAD_SIZE
    whole_ids = lax.all_gather(segment_ids, "cp", axis=1, tiled=True)[0]
    every_length = whole_ids.shape[0]
    offset = lax.axis_index("cp") * row_span
    key_index = jnp.arange(every_length, dtype=jnp.int32)
    key_positions = doc_positions(whole_ids)
    query_index = offset + jnp.arange(row_span, dtype=jnp.int32)
    query_positions = lax.dynamic_slice_in_dim(key_positions, offset, row_span)
    local_ids = segment_ids[0]
    visible = (whole_ids[None, :] == local_ids[:, None]) & (
        key_index[None, :] <= query_index[:, None]
    )
    query_cosine, query_sine = rope_tables(query_positions)
    k_cos, k_sin = rope_tables(key_positions)
    gain_a, qkv_full, out_full = (
        lax.all_gather(attn_gain, "fsdp", axis=0, tiled=True),
        lax.all_gather(w_qkv, "fsdp", axis=0, tiled=True),
        lax.all_gather(w_out, "fsdp", axis=0, tiled=True),
    )
    normed1, inv_rms1, xn = norm_forward(residual, gain_a)
    output_projection = jnp.dot(xn, qkv_full, preferred_element_type=jnp.float32)
    query_rows = apply_rotation(
        output_projection[:, :query_columns].reshape(row_span, QUERY_HEADS, HEAD_SIZE),
        query_cosine,
        query_sine,
        1.0,
    ).astype(jnp.bfloat16)
    keys_local = (
        apply_rotation(
            output_projection[:, query_columns : query_columns + key_columns].reshape(
                row_span, KEY_VALUE_HEADS, HEAD_SIZE
            ),
            query_cosine,
            query_sine,
            1.0,
        )
        .astype(jnp.bfloat16)
        .reshape(row_span, key_columns)
    )
    values_local = output_projection[:, query_columns + key_columns :].astype(jnp.bfloat16)
    every_key, every_value = (
        lax.all_gather(keys_local, "cp", axis=0, tiled=True),
        lax.all_gather(values_local, "cp", axis=0, tiled=True),
    )
    keys_three_axis = every_key.reshape(every_length, KEY_VALUE_HEADS, HEAD_SIZE)
    values_three_axis = every_value.reshape(every_length, KEY_VALUE_HEADS, HEAD_SIZE)
    attn_mix, log_total = attend(query_rows, keys_three_axis, values_three_axis, visible)
    mid = residual + jnp.dot(attn_mix, out_full, preferred_element_type=jnp.float32)
    gain_m, gate_full, up_full, down_full = (
        lax.all_gather(mlp_gain, "fsdp", axis=0, tiled=True),
        lax.all_gather(w_gate, "fsdp", axis=0, tiled=True),
        lax.all_gather(w_up, "fsdp", axis=0, tiled=True),
        lax.all_gather(w_down, "fsdp", axis=0, tiled=True),
    )
    normed2, inv_rms2, hidden_n = norm_forward(mid, gain_m)
    gate = jnp.dot(hidden_n, gate_full, preferred_element_type=jnp.float32)
    up_val = jnp.dot(hidden_n, up_full, preferred_element_type=jnp.float32)
    sigma = jax.nn.sigmoid(gate)
    silu_gate = gate * sigma
    act = (silu_gate * up_val).astype(jnp.bfloat16)
    block_output = (mid + jnp.dot(act, down_full, preferred_element_type=jnp.float32)).astype(
        jnp.bfloat16
    )
    cotangent = out_cotangent[0]
    d_act = times_transposed(cotangent, down_full)
    down_grad = transposed_times(act, cotangent)
    d_gate = (d_act * up_val * sigma * (1.0 + gate * (1.0 - sigma))).astype(jnp.bfloat16)
    d_up = (d_act * silu_gate).astype(jnp.bfloat16)
    gate_grad = transposed_times(hidden_n, d_gate)
    up_grad = transposed_times(hidden_n, d_up)
    d_hn = times_transposed(d_gate, gate_full) + times_transposed(d_up, up_full)
    mlp_gain_grad, d_norm2 = norm_backward(d_hn, normed2, inv_rms2, gain_m)
    d_mid = cotangent.astype(jnp.float32) + d_norm2
    d_mid_b = d_mid.astype(jnp.bfloat16)
    out_grad = transposed_times(attn_mix, d_mid_b)
    d_attn = times_transposed(d_mid_b, out_full).astype(jnp.bfloat16)
    d_queries, d_keys, d_values = attend_back(
        d_attn, attn_mix, query_rows, keys_three_axis, values_three_axis, visible, log_total
    )
    d_keys_flat = apply_rotation(d_keys, k_cos, k_sin, -1.0).reshape(every_length, key_columns)
    d_values_flat = d_values.reshape(every_length, key_columns)
    key_part, value_part = (
        lax.psum_scatter(d_keys_flat, "cp", scatter_dimension=0, tiled=True),
        lax.psum_scatter(d_values_flat, "cp", scatter_dimension=0, tiled=True),
    )
    d_proj = jnp.concatenate(
        [
            apply_rotation(d_queries, query_cosine, query_sine, -1.0).reshape(
                row_span, query_columns
            ),
            key_part,
            value_part,
        ],
        axis=1,
    ).astype(jnp.bfloat16)
    qkv_grad = transposed_times(xn, d_proj)
    d_xn = times_transposed(d_proj, qkv_full)
    attn_gain_grad, d_norm1 = norm_backward(d_xn, normed1, inv_rms1, gain_a)
    input_grad = d_mid + d_norm1
    gain_a_s, qkv_s, out_s, gain_m_s, gate_s, up_s, down_s = (
        lax.psum_scatter(attn_gain_grad, "fsdp", scatter_dimension=0, tiled=True),
        lax.psum_scatter(qkv_grad, "fsdp", scatter_dimension=0, tiled=True),
        lax.psum_scatter(out_grad, "fsdp", scatter_dimension=0, tiled=True),
        lax.psum_scatter(mlp_gain_grad, "fsdp", scatter_dimension=0, tiled=True),
        lax.psum_scatter(gate_grad, "fsdp", scatter_dimension=0, tiled=True),
        lax.psum_scatter(up_grad, "fsdp", scatter_dimension=0, tiled=True),
        lax.psum_scatter(down_grad, "fsdp", scatter_dimension=0, tiled=True),
    )
    gain_a_s, qkv_s, out_s, gain_m_s, gate_s, up_s, down_s = lax.psum(
        (gain_a_s, qkv_s, out_s, gain_m_s, gate_s, up_s, down_s), ("rep", "cp")
    )
    return (
        block_output[None],
        input_grad[None],
        gain_a_s,
        qkv_s,
        out_s,
        gain_m_s,
        gate_s,
        up_s,
        down_s,
    )


def solution(mesh):
    return jax.shard_map(
        shards,
        mesh=mesh,
        in_specs=(
            P(("fsdp", "rep"), "cp", None),
            P(("fsdp", "rep"), "cp"),
            P("fsdp"),
            P("fsdp", None),
            P("fsdp", None),
            P("fsdp"),
            P("fsdp", None),
            P("fsdp", None),
            P("fsdp", None),
            P(("fsdp", "rep"), "cp", None),
        ),
        out_specs=(
            P(("fsdp", "rep"), "cp", None),
            P(("fsdp", "rep"), "cp", None),
            P("fsdp"),
            P("fsdp", None),
            P("fsdp", None),
            P("fsdp"),
            P("fsdp", None),
            P("fsdp", None),
            P("fsdp", None),
        ),
        check_vma=False,
    )
```

profile of v0, /device:TPU:0, one launch (start us, length us, event | category | flops | bytes accessed | tf_op | source)
XLA Modules:
  0.0 467.3 jit_solution(3472920228963328475)
XLA Ops:
  10.1 5.4 %all_gather.35 = s32[1,768]{1,0:T(1,128)S(1)} all-gather(s32[1,384]{1,0:T(1,128)} %param.11), channel_id=1, replica_groups=mesh['fsdp'=8,'rep'=2,'cp'=2] {'cp'}, dimensions={1}, use_global_device_ids=true | all-gather | bytes 4608 | tf_op jit(solution)/shard_map/all_gather | solution.py:133
  20.3 16.2 %all-reduce.8 = (bf16[576]{0:T(1024)(128)(2,1)S(1)}, bf16[576]{0:T(1024)(128)(2,1)S(1)}) all-reduce(bf16[576]{0:T(1024)(128)(2,1)S(1)} %dynamic-update-slice, bf16[576]{0:T(1024)(128)(2,1)S(1)} %dynamic-update-slice.1), channel_id=1, replica_groups=mesh['fsdp'=8,'rep'=2,'cp'=2] {'fsdp'}, use_global_device_ids=true, to_apply=%add | all-reduce | flops 1152 | bytes 4608
  37.7 17.7 %all_gather.38 = bf16[576,576]{1,0:T(8,128)(2,1)S(1)} all-gather(bf16[72,576]{1,0:T(8,128)(2,1)} %param.14), channel_id=1, replica_groups=mesh['fsdp'=8,'rep'=2,'cp'=2] {'fsdp'}, dimensions={0}, use_global_device_ids=true | all-gather | bytes 746496 | tf_op jit(solution)/shard_map/all_gather | solution.py:149
  60.3 6.9 %all_gather.37 = bf16[768,192]{0,1:T(8,128)(2,1)S(1)} all-gather(bf16[384,192]{0,1:T(8,128)(2,1)S(1)} %bitcast.134), channel_id=1, replica_groups=mesh['fsdp'=8,'rep'=2,'cp'=2] {'cp'}, dimensions={0}, use_global_device_ids=true | all-gather | bytes 442368 | tf_op jit(solution)/shard_map/all_gather | solution.py:173
  67.3 6.3 %all_gather.34 = bf16[768,192]{0,1:T(8,128)(2,1)S(1)} all-gather(bf16[384,192]{0,1:T(8,128)(2,1)S(1)} %slice.73), channel_id=1, replica_groups=mesh['fsdp'=8,'rep'=2,'cp'=2] {'cp'}, dimensions={0}, use_global_device_ids=true | all-gather | bytes 442368 | tf_op jit(solution)/shard_map/all_gather | solution.py:174
  83.5 4.1 fusion.52
  87.5 5.2 %all-gather.9.cloned.1.call-done = bf16[576,1536]{1,0:T(8,128)(2,1)} async-done(((bf16[72,1536]{1,0:T(8,128)(2,1)}), bf16[576,1536]{1,0:T(8,128)(2,1)}) %all-gather.9.cloned.1.call-update) | async-done | bytes 1769488 | tf_op jit(solution)/shard_map/all_gather | solution.py:183
  92.7 4.1 fusion.53
  96.8 25.0 %all-gather.11.cloned.1.call-done = bf16[1536,576]{1,0:T(8,128)(2,1)} async-done(((bf16[192,576]{1,0:T(8,128)(2,1)}), bf16[1536,576]{1,0:T(8,128)(2,1)}) %all-gather.11.cloned.1.call-update) | async-done | bytes 1769488 | tf_op jit(solution)/shard_map/all_gather | solution.py:184
  121.8 6.0 %multiply_convert_fusion = (bf16[384,1536]{1,0:T(8,128)(2,1)S(1)}, bf16[384,1536]{1,0:T(8,128)(2,1)S(1)}, bf16[384,1536]{1,0:T(8,128)(2,1)}) fusion(f32[384,1536]{1,0:T(8,128)} %fusion.52, f32[384,1536]{1,0:T(8,128)} %fusion.53, bf16[1536,576]{1,0:T(8,128)(2,1)} %all-gather.11.cloned.1.call-done, bf16[1,384,576]{1,2,0:T(8,128)(2,1)S(1)} %copy-done.7), kind=kOutput, calls=%fused_computation.13 | convolution fusion | flops 688324608 | bytes 10469376 | tf_op jit(solution)/shard_map/dot_general | solution.py:41
  139.9 7.4 %fusion.5 = f32[3,64,768,1]{2,1,3,0:T(8,128)} fusion(bf16[384,3,3,64]{0,3,2,1:T(8,128)(2,1)S(1)} %bitcast.126, f32[3,768,384,3]{2,1,3,0:T(8,128)} %copy-done.1, f32[3,3,384]{2,1,0:T(4,128)} %copy-done.33, pred[384,768]{0,1:T(8,128)(4,1)} %copy-done.13), kind=kOutput, calls=%fused_computation.10 | convolution fusion | flops 350355456 | bytes 11957760 | tf_op jit(solution)/shard_map/kgnm,nkgd->mkd/dot_general | solution.py:101
  155.7 17.1 %reduce-scatter.12.cloned.1.call-done = f32[384,192]{0,1:T(8,128)} async-done(((f32[768,192]{0,1:T(8,128)}), f32[384,192]{0,1:T(8,128)}) %reduce-scatter.12.cloned.1.call-update) | async-done | bytes 294928 | tf_op jit(solution)/shard_map/reduce_scatter | solution.py:215
  176.2 4.2 fusion.55
  180.5 4.2 fusion.56
  185.9 4.3 fusion.28
  190.6 18.5 %reduce-scatter.22.cloned.1.call-done = f32[72,576]{1,0:T(8,128)} async-done(((f32[576,576]{1,0:T(8,128)}), f32[72,576]{1,0:T(8,128)}) %reduce-scatter.22.cloned.1.call-update) | async-done | bytes 165904
  209.0 36.8 %reduce-scatter.14.cloned.1.call-done = f32[72,960]{1,0:T(8,128)} async-done(((f32[576,960]{1,0:T(8,128)}), f32[72,960]{1,0:T(8,128)}) %reduce-scatter.14.cloned.1.call-update) | async-done | bytes 276496 | tf_op jit(solution)/shard_map/reduce_scatter | solution.py:233
  245.8 45.4 %reduce-scatter.16.cloned.1.call-done = f32[72,1536]{1,0:T(8,128)} async-done(((f32[576,1536]{1,0:T(8,128)}), f32[72,1536]{1,0:T(8,128)}) %reduce-scatter.16.cloned.1.call-update) | async-done | bytes 442384 | tf_op jit(solution)/shard_map/reduce_scatter | solution.py:236
  291.2 44.7 %reduce-scatter.18.cloned.1.call-done = f32[72,1536]{1,0:T(8,128)} async-done(((f32[576,1536]{1,0:T(8,128)}), f32[72,1536]{1,0:T(8,128)}) %reduce-scatter.18.cloned.1.call-update) | async-done | bytes 442384 | tf_op jit(solution)/shard_map/reduce_scatter | solution.py:237
  335.9 48.4 %reduce-scatter.20.cloned.1.call-done = f32[192,576]{1,0:T(8,128)} async-done(((f32[1536,576]{1,0:T(8,128)}), f32[192,576]{1,0:T(8,128)}) %reduce-scatter.20.cloned.1.call-update) | async-done | bytes 442384 | tf_op jit(solution)/shard_map/reduce_scatter | solution.py:238
  385.0 3.6 fusion.18
  389.4 14.3 %all-reduce.5 = (f32[576]{0:T(1024)S(1)}, f32[576]{0:T(1024)S(1)}) all-reduce(f32[576]{0:T(1024)S(1)} %get-tuple-element.11, f32[576]{0:T(1024)S(1)} %get-tuple-element.9), channel_id=4, replica_groups=mesh['fsdp'=8,'rep'=2,'cp'=2] {'fsdp'}, use_global_device_ids=true, to_apply=%region_11.12.clone | all-reduce | flops 1152 | bytes 9216
  403.9 10.4 %all-reduce.6 = (f32[72]{0:T(128)}, f32[72]{0:T(128)}) all-reduce(f32[72]{0:T(128)S(1)} %dynamic-slice.3, f32[72]{0:T(128)S(1)} %dynamic-slice.7), channel_id=1, replica_groups=mesh['fsdp'=8,'rep'=2,'cp'=2] {'rep','cp'}, use_global_device_ids=true, to_apply=%region_12.13 | all-reduce | flops 144 | bytes 1152 | tf_op jit(solution)/shard_map/psum | solution.py:240
  415.5 37.2 %all-reduce.11.cloned.1.call-done = (f32[72,960]{1,0:T(8,128)}, f32[72,576]{1,0:T(8,128)}, f32[72,1536]{1,0:T(8,128)}, f32[72,1536]{1,0:T(8,128)}, f32[192,576]{1,0:T(8,128)}) async-done(((f32[72,960]{1,0:T(8,128)}, f32[72,576]{1,0:T(8,128)}, f32[72,1536]{1,0:T(8,128)}, f32[72,1536]{1,0:T(8,128)}, f32[192,576]{1,0:T(8,128)}), (f32[72,960]{1,0:T(8,128)}, f32[72,576]{1,0:T(8,128)}, f32[72,1536]{1,0:T(8,128)}, ...) | async-done | bytes 1769488 | tf_op jit(solution)/shard_map/psum | solution.py:240
  (166 shorter events, 57.8 us)
Async XLA Ops:
  7.2 50.6 %copy-start.2 = (bf16[1,384,576]{1,2,0:T(8,128)(2,1)S(1)}, bf16[1,384,576]{1,2,0:T(8,128)(2,1)}, u32[]{:S(2)}) copy-start(bf16[1,384,576]{1,2,0:T(8,128)(2,1)} %param.10) | copy-start | bytes 1327108
  7.2 50.6 %all-gather.5.cloned.1.call-start = ((), (), s32[]{:S(2)}) async-start(), calls=%async_computation.7 | async-start | bytes 1327104 | tf_op jit(solution)/shard_map/all_gather | solution.py:148
  7.9 75.5 %all-gather.7.cloned.1.call-start = ((), (), s32[]{:S(2)}) async-start(), calls=%async_computation.8 | async-start | bytes 1990656 | tf_op jit(solution)/shard_map/all_gather | solution.py:182
  8.7 84.0 %all-gather.9.cloned.1.call-start = ((), (), s32[]{:S(2)}) async-start(), calls=%async_computation.9 | async-start | bytes 1990656 | tf_op jit(solution)/shard_map/all_gather | solution.py:183
  9.4 112.4 %all-gather.11.cloned.1.call-start = ((), (), s32[]{:S(2)}) async-start(), calls=%async_computation.10 | async-start | bytes 2211840 | tf_op jit(solution)/shard_map/all_gather | solution.py:184
  10.0 144.8 %reduce-scatter.10.cloned.1.call-start = ((), (), s32[]{:S(2)}) async-start(), calls=%async_computation.11 | async-start | bytes 884736 | tf_op jit(solution)/shard_map/reduce_scatter | solution.py:214
  56.4 10.8 %copy-start.22 = (f32[384,32]{0,1:T(8,128)}, f32[384,32]{0,1:T(8,128)S(1)}, u32[]{:S(2)}) copy-start(f32[384,32]{0,1:T(8,128)S(1)} %get-tuple-element.41) | copy-start | bytes 147460
  57.7 20.0 %copy-start.13 = (pred[384,768]{0,1:T(8,128)(4,1)}, pred[384,768]{0,1:T(8,128)(4,1)S(1)}, u32[]{:S(2)}) copy-start(pred[384,768]{0,1:T(8,128)(4,1)S(1)} %fusion.19) | copy-start | bytes 884740
  67.2 8.2 %copy-start.11 = (bf16[768,192]{0,1:T(8,128)(2,1)}, bf16[768,192]{0,1:T(8,128)(2,1)S(1)}, u32[]{:S(2)}) copy-start(bf16[768,192]{0,1:T(8,128)(2,1)S(1)} %all_gather.37) | copy-start | bytes 884740
  67.3 8.1 %copy-start.18 = (bf16[384,9,32]{0,2,1:T(8,128)(2,1)}, bf16[384,9,32]{0,2,1:T(8,128)(2,1)S(1)}, u32[]{:S(2)}) copy-start(bf16[384,9,32]{0,2,1:T(8,128)(2,1)S(1)} %get-tuple-element.29) | copy-start | bytes 663556
  67.3 8.1 %copy-start.20 = (bf16[384,9,32]{0,2,1:T(8,128)(2,1)}, bf16[384,9,32]{0,2,1:T(8,128)(2,1)S(1)}, u32[]{:S(2)}) copy-start(bf16[384,9,32]{0,2,1:T(8,128)(2,1)S(1)} %get-tuple-element.30) | copy-start | bytes 663556
  83.3 49.6 %copy-start.33 = (f32[3,3,384]{2,1,0:T(4,128)}, f32[3,3,384]{2,1,0:T(4,128)S(1)}, u32[]{:S(2)}) copy-start(f32[3,3,384]{2,1,0:T(4,128)S(1)} %log_add_fusion) | copy-start | bytes 41476
  87.5 34.3 %copy-start.7 = (bf16[1,384,576]{1,2,0:T(8,128)(2,1)S(1)}, bf16[1,384,576]{1,2,0:T(8,128)(2,1)}, u32[]{:S(2)}) copy-start(bf16[1,384,576]{1,2,0:T(8,128)(2,1)} %param.19) | copy-start | bytes 1327108
  121.8 11.0 %slice-start = ((s8[10616832]{0:T(1024)(128)(4,1)}), s8[4194304]{0:T(1024)(128)(4,1)S(1)}, s32[]{:S(2)}) async-start(s8[10616832]{0:T(1024)(128)(4,1)} %bitcast.117), calls=%async_computation.19 | async-start | bytes 8388608
  121.8 11.0 %slice-start.1 = ((s8[10616832]{0:T(1024)(128)(4,1)}), s8[4194304]{0:T(1024)(128)(4,1)S(1)}, s32[]{:S(2)}) async-start(s8[10616832]{0:T(1024)(128)(4,1)} %bitcast.117), calls=%async_computation.20 | async-start | bytes 8388608
  139.8 7.6 %copy-start.5 = (bf16[3,64,3,384]{3,1,2,0:T(8,128)(2,1)S(1)}, bf16[3,64,3,384]{3,1,2,0:T(8,128)(2,1)}, u32[]{:S(2)}) copy-start(bf16[3,64,3,384]{3,1,2,0:T(8,128)(2,1)} %copy-done.3) | copy-start | bytes 1327108
  139.8 33.0 %reduce-scatter.12.cloned.1.call-start = ((), (), s32[]{:S(2)}) async-start(), calls=%async_computation.12 | async-start | bytes 884736 | tf_op jit(solution)/shard_map/reduce_scatter | solution.py:215
  147.4 61.7 %reduce-scatter.22.cloned.1.call-start = ((), (), s32[]{:S(2)}) async-start(), calls=%async_computation.17 | async-start | bytes 1658880
  149.3 96.5 %reduce-scatter.14.cloned.1.call-start = ((), (), s32[]{:S(2)}) async-start(), calls=%async_computation.13 | async-start | bytes 2654208 | tf_op jit(solution)/shard_map/reduce_scatter | solution.py:233
  153.1 23.1 %copy-start.25 = (bf16[384,9,64]{0,2,1:T(8,128)(2,1)}, bf16[384,9,64]{0,2,1:T(8,128)(2,1)S(1)}, u32[]{:S(2)}) copy-start(bf16[384,9,64]{0,2,1:T(8,128)(2,1)S(1)} %pad_maximum_fusion.3) | copy-start | bytes 1327108
  176.2 115.1 %reduce-scatter.16.cloned.1.call-start = ((), (), s32[]{:S(2)}) async-start(), calls=%async_computation.14 | async-start | bytes 3981312 | tf_op jit(solution)/shard_map/reduce_scatter | solution.py:236
  180.4 155.4 %reduce-scatter.18.cloned.1.call-start = ((), (), s32[]{:S(2)}) async-start(), calls=%async_computation.15 | async-start | bytes 3981312 | tf_op jit(solution)/shard_map/reduce_scatter | solution.py:237
  184.7 199.6 %reduce-scatter.20.cloned.1.call-start = ((), (), s32[]{:S(2)}) async-start(), calls=%async_computation.16 | async-start | bytes 4423680 | tf_op jit(solution)/shard_map/reduce_scatter | solution.py:238
  190.3 262.4 %all-reduce.11.cloned.1.call-start = ((), (), s32[]{:S(2)}) async-start(), calls=%async_computation.18 | async-start | bytes 3710976 | tf_op jit(solution)/shard_map/psum | solution.py:240
  (27 other events, 74.6 us)
Sparse Core Ops, SparseCore 0:
  9.7 25.5 all-gather.4
  36.9 27.6 all-gather.6
  66.2 26.4 all-gather.8
  94.2 27.5 all-gather.10
  139.9 14.7 reduce-scatter.9
  157.5 15.2 reduce-scatter.11
  175.1 33.8 reduce-scatter.21
  211.3 34.4 reduce-scatter.13
  248.1 43.0 reduce-scatter.15
  293.5 42.3 reduce-scatter.17
  338.2 46.0 reduce-scatter.19
  387.8 64.8 all-reduce.10
where the time goes:
time: 468 us; the launch traced here: 467 us
  waiting for transfers between devices  283 us (60%)
  blocking collectives  77.3 us (17%)
  matrix products  62.4 us (13%)
  local copies, waits for them, and re-layouts  16.2 us (3%)
  between operations  16.1 us (3%)
  other arithmetic  11.7 us (2%)
    reduce_scatter x1, waiting for transfers between devices, shards(): lax.psum_scatter(down_grad, 'fsdp', scatter_dimension=0, tiled=True)  48.4 us
    reduce_scatter x1, waiting for transfers between devices, shards(): lax.psum_scatter(gate_grad, 'fsdp', scatter_dimension=0, tiled=True)  45.4 us
    reduce_scatter x1, waiting for transfers between devices, shards(): lax.psum_scatter(up_grad, 'fsdp', scatter_dimension=0, tiled=True)  44.7 us
    psum x1, waiting for transfers between devices, shards(): lax.psum((gain_a_s, qkv_s, out_s, gain_m_s, gate_s, up_s, down_s), ('rep'...  37.2 us
    reduce_scatter x1, waiting for transfers between devices, shards(): lax.psum_scatter(qkv_grad, 'fsdp', scatter_dimension=0, tiled=True)  36.8 us
    unnamed x2, blocking collectives  30.5 us
    all_gather x1, waiting for transfers between devices, shards(): lax.all_gather(w_down, 'fsdp', axis=0, tiled=True)  25 us
    unnamed x13, waiting for transfers between devices  21.2 us
  transfers between devices with their start and end apart: 12, of which 10 were waited for; matrix products, arithmetic and copies ran while one was open for 13% of the time, Pallas kernels for 0%

commit v1 on v0

--- a/solution.py
+++ b/solution.py
@@ -1,6 +1,10 @@
+import functools
+
 import jax
 import jax.numpy as jnp
 from jax import lax
+from jax.experimental import pallas as pl
+from jax.experimental.pallas import tpu as pltpu
 from jax.sharding import PartitionSpec as P
 
 QUERY_HEADS = 9
@@ -11,6 +15,284 @@
 EPS = 1e-05
 THETA = 100000.0
 MASKED = -1e30
+
+VMEM_BYTES = 50 * 1024 * 1024
+MESH_ID = pl.DeviceIdType.MESH
+
+
+def gather_kernel(depth, count, *refs):
+    ins, outs = refs[:count], refs[count : 2 * count]
+    own_sem, up_sem, down_sem, arrive_sem, core_sem, core_arrive = refs[2 * count :]
+    me = lax.axis_index("fsdp")
+    z, core = me // 2, me % 2
+    partner = 2 * z + 1 - core
+    barrier = pltpu.get_barrier_semaphore()
+    pl.semaphore_signal(barrier, inc=1, device_id={"fsdp": partner}, device_id_type=MESH_ID)
+
+    @pl.when(z > 0)
+    def _():
+        pl.semaphore_signal(barrier, inc=1, device_id={"fsdp": me - 2}, device_id_type=MESH_ID)
+
+    @pl.when(z < depth - 1)
+    def _():
+        pl.semaphore_signal(barrier, inc=1, device_id={"fsdp": me + 2}, device_id_type=MESH_ID)
+
+    has_down, has_up = jnp.where(z > 0, 1, 0), jnp.where(z < depth - 1, 1, 0)
+    pl.semaphore_wait(barrier, 1 + has_down + has_up)
+
+    def own(k):
+        return pltpu.make_async_copy(ins[k], outs[k].at[me], own_sem.at[k])
+
+    def along(k, shard, step, sems, source=None):
+        place = outs[k].at[2 * shard + core]
+        return pltpu.make_async_remote_copy(
+            src_ref=place if source is None else source,
+            dst_ref=place,
+            send_sem=sems.at[k, shard],
+            recv_sem=arrive_sem.at[k, shard],
+            device_id={"fsdp": me + 2 * step},
+            device_id_type=MESH_ID,
+        )
+
+    def across(k, shard, parity, source=None):
+        place = outs[k].at[2 * shard + parity]
+        return pltpu.make_async_remote_copy(
+            src_ref=place if source is None else source,
+            dst_ref=place,
+            send_sem=core_sem.at[k, shard],
+            recv_sem=core_arrive.at[k, shard],
+            device_id={"fsdp": partner},
+            device_id_type=MESH_ID,
+        )
+
+    for k in range(count):
+        own(k).start()
+
+        @pl.when(z < depth - 1)
+        def _():
+            along(k, z, 1, up_sem, ins[k]).start()
+
+        @pl.when(z > 0)
+        def _():
+            along(k, z, -1, down_sem, ins[k]).start()
+
+        across(k, z, core, ins[k]).start()
+    for k in range(count):
+        for step in range(1, depth):
+            below, above = z - step, z + step
+
+            @pl.when(below >= 0)
+            def _():
+                along(k, below, 1, up_sem).wait_recv()
+
+                @pl.when(z < depth - 1)
+                def _():
+                    along(k, below, 1, up_sem).start()
+
+                across(k, below, core).start()
+
+            @pl.when(above < depth)
+            def _():
+                along(k, above, -1, down_sem).wait_recv()
+
+                @pl.when(z > 0)
+                def _():
+                    along(k, above, -1, down_sem).start()
+
+                across(k, above, core).start()
+
+    for k in range(count):
+        own(k).wait()
+        for shard in range(depth):
+            across(k, shard, 1 - core).wait_recv()
+            across(k, shard, core).wait_send()
+
+            @pl.when((shard <= z) & (z < depth - 1))
+            def _():
+                along(k, shard, 1, up_sem).wait_send()
+
+            @pl.when((shard >= z) & (z > 0))
+            def _():
+                along(k, shard, -1, down_sem).wait_send()
+
+
+def gather_shards(arrays, ways):
+    count, depth = len(arrays), ways // 2
+    return pl.pallas_call(
+        functools.partial(gather_kernel, depth, count),
+        out_shape=[jax.ShapeDtypeStruct((ways,) + a.shape, a.dtype) for a in arrays],
+        in_specs=[pl.BlockSpec(memory_space=pltpu.VMEM)] * count,
+        out_specs=[pl.BlockSpec(memory_space=pltpu.VMEM)] * count,
+        scratch_shapes=[pltpu.SemaphoreType.DMA((count,))]
+        + [pltpu.SemaphoreType.DMA((count, depth))] * 5,
+        compiler_params=pltpu.CompilerParams(
+            collective_id=1, has_side_effects=True, vmem_limit_bytes=VMEM_BYTES
+        ),
+    )(*arrays)
+
+
+def part_of(ref, lead, index, parts):
+    rows, columns = ref.shape[-2:]
+    if columns % (4 * 128) == 0:
+        size = columns // parts
+        return ref.at[lead, :, pl.ds(pl.multiple_of(index * size, size), size)]
+    size = rows // parts
+    return ref.at[lead, pl.ds(pl.multiple_of(index * size, size), size), :]
+
+
+def reduce_kernel(depth, count, *refs):
+    parts, outs = refs[:count], refs[count : 2 * count]
+    rest = refs[2 * count :]
+    first, second, third, fourth, held, quarter, joined = [
+        rest[i * count : (i + 1) * count] for i in range(7)
+    ]
+    send0, recv0, send1, recv1, send2, recv2, send3, recv3, send4, recv4 = rest[7 * count :]
+    me, x, y = lax.axis_index("fsdp"), lax.axis_index("cp"), lax.axis_index("rep")
+    z, core = me // 2, me % 2
+    partner = 2 * z + 1 - core
+    f32 = jnp.float32
+
+    barrier = pltpu.get_barrier_semaphore()
+    others = [{"fsdp": partner}, {"cp": 1 - x}, {"rep": 1 - y}, {"cp": 1 - x, "rep": 1 - y}]
+    others += [{"fsdp": 2 * ((z + s) % depth) + core} for s in range(1, depth)]
+    for other in others:
+        pl.semaphore_signal(barrier, inc=1, device_id=other, device_id_type=MESH_ID)
+    pl.semaphore_wait(barrier, len(others))
+
+    def remote(source, place, send, recv, device):
+        return pltpu.make_async_remote_copy(
+            src_ref=source,
+            dst_ref=place,
+            send_sem=send,
+            recv_sem=recv,
+            device_id=device,
+            device_id_type=MESH_ID,
+        )
+
+    def copy0(k, j):
+        return remote(
+            parts[k].at[2 * j + 1 - core],
+            first[k].at[j],
+            send0.at[k, j],
+            recv0.at[k, j],
+            {"fsdp": partner},
+        )
+
+    def axes(j):
+        return (x, y, "cp", "rep") if j % 2 == 0 else (y, x, "rep", "cp")
+
+    def copy1(k, j):
+        own1, _, name1, _ = axes(j)
+        return remote(
+            part_of(held[k], j, 1 - own1, 2),
+            second[k].at[j],
+            send1.at[k, j],
+            recv1.at[k, j],
+            {name1: 1 - own1},
+        )
+
+    def copy2(k, j):
+        own1, own2, _, name2 = axes(j)
+        return remote(
+            part_of(held[k], j, own1 * 2 + 1 - own2, 4),
+            third[k].at[j],
+            send2.at[k, j],
+            recv2.at[k, j],
+            {name2: 1 - own2},
+        )
+
+    def copy3(k, step):
+        to = (z + step) % depth
+        return remote(
+            quarter[k].at[to],
+            fourth[k].at[step],
+            send3.at[k, step],
+            recv3.at[k, step],
+            {"fsdp": 2 * to + core},
+        )
+
+    mine = jnp.where(z % 2 == 0, x * 2 + y, y * 2 + x)
+
+    def copy4(k, which):
+        place = part_of(joined[k], 0, mine, 4)
+        device = [{"cp": 1 - x}, {"rep": 1 - y}, {"cp": 1 - x, "rep": 1 - y}][which]
+        return remote(place, place, send4.at[k, which], recv4.at[k, which], device)
+
+    for k in range(count):
+        for j in range(depth):
+            copy0(k, j).start()
+    for k in range(count):
+        for j in range(depth):
+            copy0(k, j).wait_recv()
+            total = parts[k][2 * j + core].astype(f32) + first[k][j].astype(f32)
+            held[k][j] = total.astype(held[k].dtype)
+            copy1(k, j).start()
+    for k in range(count):
+        for j in range(depth):
+            own1, own2, _, _ = axes(j)
+            copy1(k, j).wait_recv()
+            half = part_of(held[k], j, own1, 2)
+            half[...] = (half[...].astype(f32) + second[k][j].astype(f32)).astype(half.dtype)
+            copy2(k, j).start()
+    for k in range(count):
+        for j in range(depth):
+            own1, own2, _, _ = axes(j)
+            copy2(k, j).wait_recv()
+            piece = part_of(held[k], j, own1 * 2 + own2, 4)
+            total = piece[...].astype(f32) + third[k][j].astype(f32)
+            quarter[k][j] = total.astype(quarter[k].dtype)
+        for step in range(1, depth):
+            copy3(k, step).start()
+    for k in range(count):
+        total = quarter[k][z].astype(f32)
+        for step in range(1, depth):
+            copy3(k, step).wait_recv()
+            total = total + fourth[k][step].astype(f32)
+        place = part_of(joined[k], 0, mine, 4)
+        place[...] = total.astype(place.dtype)
+        for which in range(3):
+            copy4(k, which).start()
+    for k in range(count):
+        for which in range(3):
+            copy4(k, which).wait_recv()
+        outs[k][...] = joined[k][0].astype(f32)
+    for k in range(count):
+        for j in range(depth):
+            copy0(k, j).wait_send()
+            copy1(k, j).wait_send()
+            copy2(k, j).wait_send()
+        for step in range(1, depth):
+            copy3(k, step).wait_send()
+        for which in range(3):
+            copy4(k, which).wait_send()
+
+
+def reduce_shards(arrays):
+    count, ways = len(arrays), arrays[0].shape[0]
+    depth = ways // 2
+    kind = arrays[0].dtype
+    wholes = [(depth,) + a.shape[1:] for a in arrays]
+    halves, quarters = [], []
+    for a in arrays:
+        rows, columns = a.shape[1:]
+        by_columns = columns % (4 * 128) == 0
+        halves.append((depth, rows, columns // 2) if by_columns else (depth, rows // 2, columns))
+        quarters.append((depth, rows, columns // 4) if by_columns else (depth, rows // 4, columns))
+    buffers = []
+    for shapes in (wholes, halves, quarters, quarters, wholes, quarters):
+        buffers += [pltpu.VMEM(s, kind) for s in shapes]
+    buffers += [pltpu.VMEM((1,) + a.shape[1:], kind) for a in arrays]
+    sems = [pltpu.SemaphoreType.DMA((count, depth))] * 8 + [pltpu.SemaphoreType.DMA((count, 3))] * 2
+    return pl.pallas_call(
+        functools.partial(reduce_kernel, depth, count),
+        out_shape=[jax.ShapeDtypeStruct(a.shape[1:], jnp.float32) for a in arrays],
+        in_specs=[pl.BlockSpec(memory_space=pltpu.VMEM)] * count,
+        out_specs=[pl.BlockSpec(memory_space=pltpu.VMEM)] * count,
+        scratch_shapes=buffers + sems,
+        compiler_params=pltpu.CompilerParams(
+            collective_id=2, has_side_effects=True, vmem_limit_bytes=VMEM_BYTES
+        ),
+    )(*arrays)
 
 
 def rope_tables(positions):
@@ -123,14 +405,34 @@
     return (d_queries.reshape(row_span, QUERY_HEADS, HEAD_SIZE), d_keys, d_values)
 
 
+def swap_halves(value):
+    return lax.ppermute(value, "cp", [(0, 1), (1, 0)])
+
+
+def both_halves(value, axis):
+    other = swap_halves(value)
+    first = lax.axis_index("cp") == 0
+    return jnp.concatenate(
+        [jnp.where(first, value, other), jnp.where(first, other, value)], axis=axis
+    )
+
+
 def shards(
-    block_input, segment_ids, attn_gain, w_qkv, w_out, mlp_gain, w_gate, w_up, w_down, out_cotangent
+    ways, copies, block_input, segment_ids, attn_gain, w_qkv, w_out, mlp_gain, w_gate, w_up, w_down, out_cotangent
 ):
     residual = block_input[0].astype(jnp.float32)
     row_span = residual.shape[0]
     query_columns = QUERY_HEADS * HEAD_SIZE
     key_columns = KEY_VALUE_HEADS * HEAD_SIZE
-    whole_ids = lax.all_gather(segment_ids, "cp", axis=1, tiled=True)[0]
+    gains = jnp.zeros((16, 128), jnp.bfloat16)
+    gains = gains.at[0, : attn_gain.shape[0]].set(attn_gain).at[1, : mlp_gain.shape[0]].set(mlp_gain)
+    gathered = gather_shards([w_qkv, w_out, gains, w_gate, w_up, w_down], ways)
+    qkv_full, out_full, gate_full, up_full, down_full = [
+        gathered[i].reshape(-1, gathered[i].shape[-1]) for i in (0, 1, 3, 4, 5)
+    ]
+    gain_a = gathered[2][:, 0, : attn_gain.shape[0]].reshape(-1)
+    gain_m = gathered[2][:, 1, : mlp_gain.shape[0]].reshape(-1)
+    whole_ids = both_halves(segment_ids, 1)[0]
     every_length = whole_ids.shape[0]
     offset = lax.axis_index("cp") * row_span
     key_index = jnp.arange(every_length, dtype=jnp.int32)
@@ -143,11 +445,6 @@
     )
     query_cosine, query_sine = rope_tables(query_positions)
     k_cos, k_sin = rope_tables(key_positions)
-    gain_a, qkv_full, out_full = (
-        lax.all_gather(attn_gain, "fsdp", axis=0, tiled=True),
-        lax.all_gather(w_qkv, "fsdp", axis=0, tiled=True),
-        lax.all_gather(w_out, "fsdp", axis=0, tiled=True),
-    )
     normed1, inv_rms1, xn = norm_forward(residual, gain_a)
     output_projection = jnp.dot(xn, qkv_full, preferred_element_type=jnp.float32)
     query_rows = apply_rotation(
@@ -169,20 +466,12 @@
         .reshape(row_span, key_columns)
     )
     values_local = output_projection[:, query_columns + key_columns :].astype(jnp.bfloat16)
-    every_key, every_value = (
-        lax.all_gather(keys_local, "cp", axis=0, tiled=True),
-        lax.all_gather(values_local, "cp", axis=0, tiled=True),
-    )
+    every_pair = both_halves(jnp.concatenate([keys_local, values_local], axis=1), 0)
+    every_key, every_value = every_pair[:, :key_columns], every_pair[:, key_columns:]
     keys_three_axis = every_key.reshape(every_length, KEY_VALUE_HEADS, HEAD_SIZE)
     values_three_axis = every_value.reshape(every_length, KEY_VALUE_HEADS, HEAD_SIZE)
     attn_mix, log_total = attend(query_rows, keys_three_axis, values_three_axis, visible)
     mid = residual + jnp.dot(attn_mix, out_full, preferred_element_type=jnp.float32)
-    gain_m, gate_full, up_full, down_full = (
-        lax.all_gather(mlp_gain, "fsdp", axis=0, tiled=True),
-        lax.all_gather(w_gate, "fsdp", axis=0, tiled=True),
-        lax.all_gather(w_up, "fsdp", axis=0, tiled=True),
-        lax.all_gather(w_down, "fsdp", axis=0, tiled=True),
-    )
     normed2, inv_rms2, hidden_n = norm_forward(mid, gain_m)
     gate = jnp.dot(hidden_n, gate_full, preferred_element_type=jnp.float32)
     up_val = jnp.dot(hidden_n, up_full, preferred_element_type=jnp.float32)
@@ -210,17 +499,17 @@
     )
     d_keys_flat = apply_rotation(d_keys, k_cos, k_sin, -1.0).reshape(every_length, key_columns)
     d_values_flat = d_values.reshape(every_length, key_columns)
-    key_part, value_part = (
-        lax.psum_scatter(d_keys_flat, "cp", scatter_dimension=0, tiled=True),
-        lax.psum_scatter(d_values_flat, "cp", scatter_dimension=0, tiled=True),
-    )
+    pair = jnp.concatenate([d_keys_flat, d_values_flat], axis=1)
+    away = lax.dynamic_slice_in_dim(pair, row_span - offset, row_span)
+    pair_part = lax.dynamic_slice_in_dim(pair, offset, row_span) + swap_halves(
+        away.astype(jnp.bfloat16)
+    ).astype(jnp.float32)
     d_proj = jnp.concatenate(
         [
             apply_rotation(d_queries, query_cosine, query_sine, -1.0).reshape(
                 row_span, query_columns
             ),
-            key_part,
-            value_part,
+            pair_part,
         ],
         axis=1,
     ).astype(jnp.bfloat16)
@@ -228,18 +517,25 @@
     d_xn = times_transposed(d_proj, qkv_full)
     attn_gain_grad, d_norm1 = norm_backward(d_xn, normed1, inv_rms1, gain_a)
     input_grad = d_mid + d_norm1
-    gain_a_s, qkv_s, out_s, gain_m_s, gate_s, up_s, down_s = (
-        lax.psum_scatter(attn_gain_grad, "fsdp", scatter_dimension=0, tiled=True),
-        lax.psum_scatter(qkv_grad, "fsdp", scatter_dimension=0, tiled=True),
-        lax.psum_scatter(out_grad, "fsdp", scatter_dimension=0, tiled=True),
-        lax.psum_scatter(mlp_gain_grad, "fsdp", scatter_dimension=0, tiled=True),
-        lax.psum_scatter(gate_grad, "fsdp", scatter_dimension=0, tiled=True),
-        lax.psum_scatter(up_grad, "fsdp", scatter_dimension=0, tiled=True),
-        lax.psum_scatter(down_grad, "fsdp", scatter_dimension=0, tiled=True),
-    )
-    gain_a_s, qkv_s, out_s, gain_m_s, gate_s, up_s, down_s = lax.psum(
-        (gain_a_s, qkv_s, out_s, gain_m_s, gate_s, up_s, down_s), ("rep", "cp")
-    )
+    if copies == (2, 2):
+        bf16 = jnp.bfloat16
+        shard = attn_gain.shape[0]
+        gain_grads = jnp.stack(
+            [attn_gain_grad.reshape(ways, shard), mlp_gain_grad.reshape(ways, shard)], axis=1
+        )
+        gain_grads = jnp.pad(gain_grads, ((0, 0), (0, 14), (0, 512 - shard))).astype(bf16)
+        both = jnp.concatenate([qkv_grad.astype(bf16), out_grad.astype(bf16)], axis=1)
+        stacked = [
+            g.astype(bf16).reshape(ways, -1, g.shape[-1])
+            for g in (gate_grad, up_grad, down_grad, both)
+        ]
+        gate_s, up_s, down_s, both_s, gain_s = reduce_shards(stacked + [gain_grads])
+        qkv_s, out_s = both_s[:, : w_qkv.shape[1]], both_s[:, w_qkv.shape[1] :]
+        gain_a_s, gain_m_s = gain_s[0, :shard], gain_s[1, :shard]
+    else:
+        grads = (attn_gain_grad, qkv_grad, out_grad, mlp_gain_grad, gate_grad, up_grad, down_grad)
+        grads = [lax.psum_scatter(g, "fsdp", scatter_dimension=0, tiled=True) for g in grads]
+        gain_a_s, qkv_s, out_s, gain_m_s, gate_s, up_s, down_s = lax.psum(grads, ("rep", "cp"))
     return (
         block_output[None],
         input_grad[None],
@@ -254,8 +550,10 @@
 
 
 def solution(mesh):
+    ways = mesh.shape["fsdp"]
+    copies = (mesh.shape["rep"], mesh.shape["cp"])
     return jax.shard_map(
-        shards,
+        functools.partial(shards, ways, copies),
         mesh=mesh,
         in_specs=(
             P(("fsdp", "rep"), "cp", None),

time: 468 us -> 214 us (0.46)
  waiting for transfers between devices: 283 us -> 9.37 us
  Pallas kernels: 0 us -> 125 us
  blocking collectives: 77.3 us -> 0 us
  matrix products: 62.4 us -> 40.9 us
  between operations: 16.1 us -> 1.05 us
    reduce_scatter x6 -> x0, waiting for transfers between devices: 194 us -> none  [the longest x1 48.4 us: shards(): lax.psum_scatter(down_grad, 'fsdp', scatter_dimension=0, tiled=True)]
    pallas_call x0 -> x2, Pallas kernels: none -> 125 us  [the longest x1 69 us: gather_shards(): pl.pallas_call(functools.partial(gather_kernel, depth, count), out_shape=...]
    psum x1 -> x0, waiting for transfers between devices: 37.2 us -> none  [shards(): lax.psum((gain_a_s, qkv_s, out_s, gain_m_s, gate_s, up_s, down_s), ('rep'...]
    all_gather x4 -> x0, blocking collectives: 36.4 us -> none  [the longest x1 17.7 us: shards(): lax.all_gather(w_out, 'fsdp', axis=0, tiled=True)]
    unnamed x2 -> x0, blocking collectives: 30.5 us -> none
    all_gather x4 -> x0, waiting for transfers between devices: 30.3 us -> none  [the longest x1 25 us: shards(): lax.all_gather(w_down, 'fsdp', axis=0, tiled=True)]
    unnamed x13 -> x0, waiting for transfers between devices: 21.2 us -> none
    psum x1 -> x0, blocking collectives: 10.4 us -> none  [shards(): lax.psum((gain_a_s, qkv_s, out_s, gain_m_s, gate_s, up_s, down_s), ('rep'...]
  transfers between devices with their start and end apart: 12 -> 3, of which waited for: 10 -> 2; matrix products, arithmetic and copies ran while one was open for 13% -> 8% of each run, Pallas kernels for 0% -> 32%
where the time goes in v1:
time: 214 us; the launch traced here: 213 us
  Pallas kernels  125 us (58%)
  matrix products  40.9 us (19%)
  local copies, waits for them, and re-layouts  20.4 us (10%)
  other arithmetic  12 us (6%)
  waiting for transfers between devices  9.37 us (4%)
  starting transfers between devices  4.16 us (2%)
    pallas_call x1, Pallas kernels, gather_shards(): pl.pallas_call(functools.partial(gather_kernel, depth, count), out_shape=...  69 us
    pallas_call x1, Pallas kernels, reduce_shards(): pl.pallas_call(functools.partial(reduce_kernel, depth, count), out_shape=...  56.2 us
    dot_general x5, matrix products, transposed_times(): lax.dot_general(left, right, (((0,), (0,)), ((), ())), preferred_element_...  10.6 us
    unnamed x55, local copies, waits for them, and re-layouts  9.58 us
    ppermute x3, waiting for transfers between devices, swap_halves(): return lax.ppermute(value, 'cp', [(0, 1), (1, 0)])  9.37 us
    dot_general x5, matrix products, times_transposed(): lax.dot_general(left, right, (((1,), (1,)), ((), ())), preferred_element_...  7.69 us
  transfers between devices with their start and end apart: 3, of which 2 were waited for; matrix products, arithmetic and copies ran while one was open for 8% of the time, Pallas kernels for 32%

profile of v1, /device:TPU:0, one launch (start us, length us, event | category | flops | bytes accessed | tf_op | source)
XLA Modules:
  0.0 213.1 jit_solution(17359371677136561007)
XLA Ops:
  0.6 3.0 %collective-permute-start = (s32[1,384]{1,0:T(1,128)}, s32[1,384]{1,0:T(1,128)S(1)}, u32[]{:S(2)}, u32[]{:S(2)}) collective-permute-start(s32[1,384]{1,0:T(1,128)} %param.15), channel_id=1, source_target_pairs={{0,1},{1,0},{2,3},{3,2},{4,5},{5,4},{6,7},{7,6},{8,9},{9,8},{10,11... | collective-permute-start | bytes 4616 | tf_op jit(solution)/shard_map/ppermute | solution.py:409
  9.7 69.0 %shard_map.169 = (bf16[8,72,960]{2,1,0:T(8,128)(2,1)S(1)}, bf16[8,72,576]{2,1,0:T(8,128)(2,1)S(1)}, bf16[8,16,128]{2,1,0:T(8,128)(2,1)S(1)}, bf16[8,72,1536]{2,1...) custom-call(bf16[72,960]{1,0:T(8,128)(2,1)S(1)} %copy-done.3, ...), custom_call_target="tpu_custom_call" | custom-call | tf_op jit(solution)/shard_map/pallas_call | solution.py:121
  80.0 3.1 %fusion.39 = f32[384,960]{0,1:T(8,128)} fusion(bf16[576,960]{1,0:T(8,128)(2,1)S(1)} %bitcast.161, bf16[1,384,576]{1,2,0:T(8,128)(2,1)} %param.14, f32[576]{0:T(1024)S(1)} %reshape.415, f32[384]{0:T(512)S(1)} %add_rsqrt_fusion.1), kind=kOutput, calls=%fused_computation.78 | convolution fusion | flops 425558016 | bytes 3026688 | tf_op jit(solution)/shard_map/dot_general | solution.py:449
  84.2 2.1 %slice.118 = f32[384,576]{0,1:T(8,128)} slice(f32[384,960]{0,1:T(8,128)} %fusion.39), slice={[0:384], [0:576]} | slice | bytes 1769472 | tf_op jit(solution)/shard_map/slice | solution.py:451
  88.8 7.9 %collective-permute-done.1 = bf16[384,384]{0,1:T(8,128)(2,1)S(1)} collective-permute-done((bf16[384,384]{0,1:T(8,128)(2,1)S(1)}, bf16[384,384]{0,1:T(8,128)(2,1)S(1)}, u32[]{:S(2)}, u32[]{:S(2)}) %collective-permute-start.1) | collective-permute-done | bytes 294944 | tf_op jit(solution)/shard_map/ppermute | solution.py:409
  96.8 1.8 fusion.4
  98.6 2.2 %fusion.2 = f32[3,3,384]{2,1,0:T(4,128)S(1)} fusion(f32[3,768,384,3]{2,1,3,0:T(8,128)S(1)} %get-tuple-element.89, f32[3,3,384]{2,1,0:T(4,128)S(1)} %get-tuple-element.88, pred[384,768]{0,1:T(8,128)(4,1)S(1)} %fusion.15), kind=kLoop, calls=%fused_computation.7 | loop fusion | flops 10613376 | bytes 10939392 | tf_op jit(solution)/shard_map/reduce_sum | solution.py:365
  100.8 2.9 %fusion.11 = bf16[3,64,3,384]{3,1,2,0:T(8,128)(2,1)S(1)} fusion(bf16[768,3,64,1]{0,2,3,1:T(8,128)(2,1)S(1)} %bitcast.188, f32[3,768,384,3]{2,1,3,0:T(8,128)S(1)} %get-tuple-element.89, f32[3,3,384]{2,1,0:T(4,128)S(1)} %fusion.2, f32[3,3,384]{2,1,0:T(4,128)S(1)} %get-tuple-element.88, pred[384,768]{0,1:T(8,128)(4,1)S(1)} %fusion.15), kind=kOutput, calls=%fused_computation.36 | convolution fusion | flops 353230848 | bytes 11676672 | tf_op jit(solution)/shard_map/kgnm,mkd->nkgd/dot_general | solution.py:368
  108.5 3.1 %multiply_convert_fusion = (bf16[384,1536]{1,0:T(8,128)(2,1)S(1)}, bf16[384,1536]{1,0:T(8,128)(2,1)S(1)}, bf16[384,1536]{1,0:T(8,128)(2,1)}) fusion(f32[384,1536]{1,0:T(8,128)S(1)} %fusion.68, f32[384,1536]{1,0:T(8,128)S(1)} %fusion.69, bf16[1536,576]{1,0:T(8,128)(2,1)S(1)} %bitcast.193, bf16[1,384,576]{1,2,0:T(8,128)(2,1)S(1)} %copy-done.16), kind=kOutput, calls=%fused_computation.17 | convolution fusion | flops 688324608 | bytes 10469376 | tf_op jit(solution)/shard_map/dot_general | solution.py:323
  115.2 2.5 %fusion.5 = f32[3,64,768,1]{2,1,3,0:T(8,128)S(1)} fusion(bf16[384,3,3,64]{0,3,2,1:T(8,128)(2,1)S(1)} %bitcast.176, f32[3,768,384,3]{2,1,3,0:T(8,128)S(1)} %get-tuple-element.89, f32[3,3,384]{2,1,0:T(4,128)S(1)} %log_add_fusion, pred[384,768]{0,1:T(8,128)(4,1)S(1)} %fusion.15), kind=kOutput, calls=%fused_computation.10 | convolution fusion | flops 350355456 | bytes 11957760 | tf_op jit(solution)/shard_map/kgnm,nkgd->mkd/dot_general | solution.py:383
  117.8 3.7 %fusion.1 = bf16[3,3,384,768]{2,3,1,0:T(8,128)(2,1)S(1)} fusion(f32[3,768,384,3]{2,1,3,0:T(8,128)S(1)} %get-tuple-element.89, f32[3,3,384]{2,1,0:T(4,128)S(1)} %bitcast.190, f32[3,3,384]{2,1,0:T(4,128)S(1)} %log_add_fusion, pred[384,768]{0,1:T(8,128)(4,1)S(1)} %fusion.15, bf16[768,3,64,1]{0,2,3,1:T(8,128)(2,1)S(1)} %bitcast.189, ...), kind=kOutput, calls=%fused_computation.2 | convolution fusion | flops 355663872 | bytes 16985088 | tf_op jit(solution)/shard_map/nkgd,mkd->kgnm/dot_general | solution.py:386
  121.5 1.9 convolution_multiply_fusion
  123.4 1.6 fusion.13
  125.1 1.5 convolution_convert_fusion.4
  126.6 2.3 %convolution_convert_fusion.1 = bf16[576,1536]{1,0:T(8,128)(2,1)} fusion(bf16[384,576]{0,1:T(8,128)(2,1)S(1)} %multiply_convert_fusion.3, bf16[384,1536]{1,0:T(8,128)(2,1)S(1)} %copy-done.23), kind=kOutput, calls=%fused_computation.14 | convolution fusion | flops 680361984 | bytes 3391488 | tf_op jit(solution)/shard_map/dot_general | solution.py:329
  128.9 2.3 %convolution_convert_fusion = bf16[1536,576]{0,1:T(8,128)(2,1)} fusion(bf16[384,1536]{1,0:T(8,128)(2,1)S(1)} %copy-done.24, bf16[1,384,576]{1,2,0:T(8,128)(2,1)S(1)} %copy-done.16), kind=kOutput, calls=%fused_computation.13 | convolution fusion | flops 680361984 | bytes 3391488 | tf_op jit(solution)/shard_map/dot_general | solution.py:329
  131.3 1.9 fusion.14
  135.5 3.9 %copy.38 = bf16[1536,576]{1,0:T(8,128)(2,1)} copy(bf16[1536,576]{0,1:T(8,128)(2,1)} %convolution_convert_fusion) | data formatting | bytes 3538944 | tf_op jit(solution)/shard_map/convert_element_type | solution.py:529
  139.6 2.6 %convolution_convert_fusion.2 = bf16[576,1536]{1,0:T(8,128)(2,1)S(1)} fusion(bf16[384,576]{0,1:T(8,128)(2,1)} %copy-done.17, bf16[384,1536]{1,0:T(8,128)(2,1)} %copy-done.25), kind=kOutput, calls=%fused_computation.15 | convolution fusion | flops 680361984 | bytes 3391488 | tf_op jit(solution)/shard_map/dot_general | solution.py:329
  142.2 1.5 collective-permute-done.2
  144.7 1.7 fusion.28
  146.5 1.9 convolution_convert_fusion.3
  148.5 2.9 %pad_maximum_fusion = bf16[576,1536]{1,0:T(8,128)(2,1)} fusion(bf16[576,576]{1,0:T(8,128)(2,1)S(1)} %copy-done.12, bf16[576,960]{1,0:T(8,128)(2,1)} %convolution_convert_fusion.3), kind=kLoop, calls=%fused_computation.23 | loop fusion | flops 3538944 | bytes 3538944 | tf_op jit(solution)/shard_map/concatenate | solution.py:527
  151.4 56.2 %shard_map.170 = (f32[72,1536]{1,0:T(8,128)S(1)}, f32[72,1536]{1,0:T(8,128)S(1)}, f32[192,576]{1,0:T(8,128)S(1)}, f32[72,1536]{1,0:T(8,128)S(1)}, f32[16,512]{1,0:T(8,128)S(1)}) custom-call(bf16[8,72,1536]{2,1,0:T(8,128)(2,1)S(1)} %bitcast.160, bf16[8,72,1536]{2,1,0:T(8,128)(2,1)} %bitcast.174, bf16[8,192,576]{2,1,0:T(8,128)(2,1)} %bitcast.163, ...), custom_call_target="tpu_custom_call" | custom-call | tf_op jit(solution)/shard_map/pallas_call | solution.py:286
  (110 shorter events, 28.3 us)
Async XLA Ops:
  0.6 85.8 %collective-permute-start = (s32[1,384]{1,0:T(1,128)}, s32[1,384]{1,0:T(1,128)S(1)}, u32[]{:S(2)}, u32[]{:S(2)}) collective-permute-start(s32[1,384]{1,0:T(1,128)} %param.15), channel_id=1, source_target_pairs={{0,1},{1,0},{2,3},{3,2},{4,5},{5,4},{6,7},{7,6},{8,9},{9,8},{10,11... | collective-permute-start | bytes 4616 | tf_op jit(solution)/shard_map/ppermute | solution.py:409
  80.0 6.4 %copy-start.18 = (s32[1,384]{1,0:T(1,128)S(1)}, s32[1,384]{1,0:T(1,128)}, u32[]{:S(2)}) copy-start(s32[1,384]{1,0:T(1,128)} %param.15) | copy-start | bytes 4612
  83.1 4.1 %slice-start = ((f32[384,960]{0,1:T(8,128)}), f32[384,192]{0,1:T(8,128)S(1)}, s32[]{:S(2)}) async-start(f32[384,960]{0,1:T(8,128)} %fusion.39), calls=%async_computation | async-start | bytes 589824 | tf_op jit(solution)/shard_map/slice | solution.py:458
  86.4 2.2 %copy-start.10 = (f32[384,576]{0,1:T(8,128)S(1)}, f32[384,576]{0,1:T(8,128)}, u32[]{:S(2)}) copy-start(f32[384,576]{0,1:T(8,128)} %slice.118) | copy-start | bytes 2654212
  87.3 9.4 %collective-permute-start.1 = (bf16[384,384]{0,1:T(8,128)(2,1)S(1)}, bf16[384,384]{0,1:T(8,128)(2,1)S(1)}, u32[]{:S(2)}, u32[]{:S(2)}) collective-permute-start(bf16[384,384]{0,1:T(8,128)(2,1)S(1)} %pad_maximum_fusion.8), channel_id=1, source_target_pairs={{0,1},{1,0},{2,3},{3,2},{4,5},{5,4},{6,7},{7,6},{8,9},{9,8},{10,11... | collective-permute-start | bytes 884744 | tf_op jit(solution)/shard_map/ppermute | solution.py:409
  100.8 3.0 %copy-start.7 = (bf16[1,384,576]{1,2,0:T(8,128)(2,1)S(1)}, bf16[1,384,576]{1,2,0:T(8,128)(2,1)}, u32[]{:S(2)}) copy-start(bf16[1,384,576]{1,2,0:T(8,128)(2,1)} %param.14) | copy-start | bytes 1327108
  103.8 1.5 copy-start.20
  104.7 22.0 %copy-start.17 = (bf16[384,576]{0,1:T(8,128)(2,1)}, bf16[384,576]{0,1:T(8,128)(2,1)S(1)}, u32[]{:S(2)}) copy-start(bf16[384,576]{0,1:T(8,128)(2,1)S(1)} %multiply_convert_fusion.3) | copy-start | bytes 1327108
  105.3 1.5 copy-start.21
  106.8 1.1 copy-start.16
  106.8 1.7 copy-start.19
  111.5 1.1 copy-start.25
  111.5 1.5 copy-start.22
  114.5 10.6 %copy-start.5 = (f32[384,576]{0,1:T(8,128)}, f32[384,576]{0,1:T(8,128)S(1)}, u32[]{:S(2)}) copy-start(f32[384,576]{0,1:T(8,128)S(1)} %multiply_add_fusion) | copy-start | bytes 2654212
  117.8 15.5 %copy-start.13 = (f32[3,64,768,1]{2,1,3,0:T(8,128)}, f32[3,64,768,1]{2,1,3,0:T(8,128)S(1)}, u32[]{:S(2)}) copy-start(f32[3,64,768,1]{2,1,3,0:T(8,128)S(1)} %fusion.5) | copy-start | bytes 1769476
  123.4 3.2 %copy-start.23 = (bf16[384,1536]{1,0:T(8,128)(2,1)S(1)}, bf16[384,1536]{1,0:T(8,128)(2,1)}, u32[]{:S(2)}) copy-start(bf16[384,1536]{1,0:T(8,128)(2,1)} %copy-done.22) | copy-start | bytes 3538948
  126.6 2.3 %copy-start.24 = (bf16[384,1536]{1,0:T(8,128)(2,1)S(1)}, bf16[384,1536]{1,0:T(8,128)(2,1)}, u32[]{:S(2)}) copy-start(bf16[384,1536]{1,0:T(8,128)(2,1)} %get-tuple-element.63) | copy-start | bytes 3538948
  134.1 5.3 %copy-start.11 = (f32[3,64,3,384]{3,1,2,0:T(8,128)S(1)}, f32[3,64,3,384]{3,1,2,0:T(8,128)}, u32[]{:S(2)}) copy-start(f32[3,64,3,384]{3,1,2,0:T(8,128)} %convolution_multiply_fusion) | copy-start | bytes 2654212
  134.9 8.8 %collective-permute-start.2 = (bf16[384,384]{0,1:T(8,128)(2,1)}, bf16[384,384]{0,1:T(8,128)(2,1)}, u32[]{:S(2)}, u32[]{:S(2)}) collective-permute-start(bf16[384,384]{0,1:T(8,128)(2,1)} %fusion.33), channel_id=1, source_target_pairs={{0,1},{1,0},{2,3},{3,2},{4,5},{5,4},{6,7},{7,6},{8,9},{9,8},{10,11... | collective-permute-start | bytes 884744 | tf_op jit(solution)/shard_map/ppermute | solution.py:409
  139.6 4.1 %copy-start.9 = (f32[768,3,64]{0,2,1:T(8,128)S(1)}, f32[768,3,64]{0,2,1:T(8,128)}, u32[]{:S(2)}) copy-start(f32[768,3,64]{0,2,1:T(8,128)} %copy-done.8) | copy-start | bytes 1769476
  139.6 4.1 %copy-start.14 = (f32[3,64,768,1]{2,1,3,0:T(8,128)S(1)}, f32[3,64,768,1]{2,1,3,0:T(8,128)}, u32[]{:S(2)}) copy-start(f32[3,64,768,1]{2,1,3,0:T(8,128)} %copy-done.13) | copy-start | bytes 1769476
  146.5 2.0 copy-start.12
  151.4 58.2 %copy-start.6 = (f32[384,576]{0,1:T(8,128)S(1)}, f32[384,576]{0,1:T(8,128)}, u32[]{:S(2)}) copy-start(f32[384,576]{0,1:T(8,128)} %copy-done.5) | copy-start | bytes 2654212
  151.4 58.2 %copy-start.15 = (f32[384,576]{0,1:T(8,128)S(1)}, f32[384,576]{0,1:T(8,128)}, u32[]{:S(2)}) copy-start(f32[384,576]{0,1:T(8,128)} %get-tuple-element.93) | copy-start | bytes 2654212
  (6 other events, 5.5 us)

commit v2 on v1

--- a/solution.py
+++ b/solution.py
@@ -18,117 +18,6 @@
 
 VMEM_BYTES = 50 * 1024 * 1024
 MESH_ID = pl.DeviceIdType.MESH
-
-
-def gather_kernel(depth, count, *refs):
-    ins, outs = refs[:count], refs[count : 2 * count]
-    own_sem, up_sem, down_sem, arrive_sem, core_sem, core_arrive = refs[2 * count :]
-    me = lax.axis_index("fsdp")
-    z, core = me // 2, me % 2
-    partner = 2 * z + 1 - core
-    barrier = pltpu.get_barrier_semaphore()
-    pl.semaphore_signal(barrier, inc=1, device_id={"fsdp": partner}, device_id_type=MESH_ID)
-
-    @pl.when(z > 0)
-    def _():
-        pl.semaphore_signal(barrier, inc=1, device_id={"fsdp": me - 2}, device_id_type=MESH_ID)
-
-    @pl.when(z < depth - 1)
-    def _():
-        pl.semaphore_signal(barrier, inc=1, device_id={"fsdp": me + 2}, device_id_type=MESH_ID)
-
-    has_down, has_up = jnp.where(z > 0, 1, 0), jnp.where(z < depth - 1, 1, 0)
-    pl.semaphore_wait(barrier, 1 + has_down + has_up)
-
-    def own(k):
-        return pltpu.make_async_copy(ins[k], outs[k].at[me], own_sem.at[k])
-
-    def along(k, shard, step, sems, source=None):
-        place = outs[k].at[2 * shard + core]
-        return pltpu.make_async_remote_copy(
-            src_ref=place if source is None else source,
-            dst_ref=place,
-            send_sem=sems.at[k, shard],
-            recv_sem=arrive_sem.at[k, shard],
-            device_id={"fsdp": me + 2 * step},
-            device_id_type=MESH_ID,
-        )
-
-    def across(k, shard, parity, source=None):
-        place = outs[k].at[2 * shard + parity]
-        return pltpu.make_async_remote_copy(
-            src_ref=place if source is None else source,
-            dst_ref=place,
-            send_sem=core_sem.at[k, shard],
-            recv_sem=core_arrive.at[k, shard],
-            device_id={"fsdp": partner},
-            device_id_type=MESH_ID,
-        )
-
-    for k in range(count):
-        own(k).start()
-
-        @pl.when(z < depth - 1)
-        def _():
-            along(k, z, 1, up_sem, ins[k]).start()
-
-        @pl.when(z > 0)
-        def _():
-            along(k, z, -1, down_sem, ins[k]).start()
-
-        across(k, z, core, ins[k]).start()
-    for k in range(count):
-        for step in range(1, depth):
-            below, above = z - step, z + step
-
-            @pl.when(below >= 0)
-            def _():
-                along(k, below, 1, up_sem).wait_recv()
-
-                @pl.when(z < depth - 1)
-                def _():
-                    along(k, below, 1, up_sem).start()
-
-                across(k, below, core).start()
-
-            @pl.when(above < depth)
-            def _():
-                along(k, above, -1, down_sem).wait_recv()
-
-                @pl.when(z > 0)
-                def _():
-                    along(k, above, -1, down_sem).start()
-
-                across(k, above, core).start()
-
-    for k in range(count):
-        own(k).wait()
-        for shard in range(depth):
-            across(k, shard, 1 - core).wait_recv()
-            across(k, shard, core).wait_send()
-
-            @pl.when((shard <= z) & (z < depth - 1))
-            def _():
-                along(k, shard, 1, up_sem).wait_send()
-
-            @pl.when((shard >= z) & (z > 0))
-            def _():
-                along(k, shard, -1, down_sem).wait_send()
-
-
-def gather_shards(arrays, ways):
-    count, depth = len(arrays), ways // 2
-    return pl.pallas_call(
-        functools.partial(gather_kernel, depth, count),
-        out_shape=[jax.ShapeDtypeStruct((ways,) + a.shape, a.dtype) for a in arrays],
-        in_specs=[pl.BlockSpec(memory_space=pltpu.VMEM)] * count,
-        out_specs=[pl.BlockSpec(memory_space=pltpu.VMEM)] * count,
-        scratch_shapes=[pltpu.SemaphoreType.DMA((count,))]
-        + [pltpu.SemaphoreType.DMA((count, depth))] * 5,
-        compiler_params=pltpu.CompilerParams(
-            collective_id=1, has_side_effects=True, vmem_limit_bytes=VMEM_BYTES
-        ),
-    )(*arrays)
 
 
 def part_of(ref, lead, index, parts):
@@ -138,6 +27,133 @@
         return ref.at[lead, :, pl.ds(pl.multiple_of(index * size, size), size)]
     size = rows // parts
     return ref.at[lead, pl.ds(pl.multiple_of(index * size, size), size), :]
+
+
+def gather_kernel(depth, count, *refs):
+    ins, outs = refs[:count], refs[count : 2 * count]
+    own_sem, z_send, z_recv, send1, recv1, send2, recv2, core_send, core_recv = refs[2 * count :]
+    me, x, y = lax.axis_index("fsdp"), lax.axis_index("cp"), lax.axis_index("rep")
+    z, core = me // 2, me % 2
+    partner = 2 * z + 1 - core
+    barrier = pltpu.get_barrier_semaphore()
+    others = [{"fsdp": partner}, {"cp": 1 - x}, {"rep": 1 - y}]
+    others += [{"fsdp": 2 * ((z + s) % depth) + core} for s in range(1, depth)]
+    for other in others:
+        pl.semaphore_signal(barrier, inc=1, device_id=other, device_id_type=MESH_ID)
+    pl.semaphore_wait(barrier, len(others))
+
+    def remote(source, place, send, recv, device):
+        return pltpu.make_async_remote_copy(
+            src_ref=source,
+            dst_ref=place,
+            send_sem=send,
+            recv_sem=recv,
+            device_id=device,
+            device_id_type=MESH_ID,
+        )
+
+    def axes(j):
+        return (x, y, "cp", "rep") if j % 2 == 0 else (y, x, "rep", "cp")
+
+    def own(k):
+        return pltpu.make_async_copy(ins[k].at[0], outs[k].at[me], own_sem.at[k])
+
+    def outward(k, step):
+        mine = jnp.where(z % 2 == 0, y * 2 + x, x * 2 + y)
+        return remote(
+            part_of(ins[k], 0, mine, 4),
+            part_of(outs[k], me, mine, 4),
+            z_send.at[k, step],
+            z_recv.at[k, step],
+            {"fsdp": 2 * ((z + step) % depth) + core},
+        )
+
+    def inward(k, step):
+        shard = (z + depth - step) % depth
+        even = shard % 2 == 0
+        mine = jnp.where(even, y * 2 + x, x * 2 + y)
+        place = part_of(outs[k], 2 * shard + core, mine, 4)
+        return remote(place, place, z_send.at[k, step], z_recv.at[k, step], {"fsdp": partner})
+
+    def joins(k, shard, which):
+        own1, own2, name1, name2 = axes(shard)
+        if which == 0:
+            quarter = part_of(outs[k], 2 * shard + core, own2 * 2 + own1, 4)
+            send, recv = send1.at[k, shard], recv1.at[k, shard]
+            return remote(quarter, quarter, send, recv, {name1: 1 - own1})
+        half = part_of(outs[k], 2 * shard + core, own2, 2)
+        send, recv = send2.at[k, shard], recv2.at[k, shard]
+        return remote(half, half, send, recv, {name2: 1 - own2})
+
+    def across(k, shard, source=None):
+        place = outs[k].at[2 * shard + core]
+        return remote(
+            place if source is None else source,
+            place,
+            core_send.at[k, shard],
+            core_recv.at[k, shard],
+            {"fsdp": partner},
+        )
+
+    for k in range(count):
+        for step in range(1, depth):
+            outward(k, step).start()
+        own(k).start()
+        across(k, z, ins[k].at[0]).start()
+
+    def arrived(k, shard):
+        step = (z + depth - shard) % depth
+
+        @pl.when(shard != z)
+        def _():
+            inward(k, step).wait_recv()
+            joins(k, shard, 0).start()
+
+    def joined(k, shard):
+        @pl.when(shard != z)
+        def _():
+            joins(k, shard, 0).wait_recv()
+            joins(k, shard, 1).start()
+
+    def complete(k, shard):
+        @pl.when(shard != z)
+        def _():
+            joins(k, shard, 1).wait_recv()
+            across(k, shard).start()
+
+    items = [(k, shard) for k in range(count) for shard in range(depth)]
+    lag = 2
+    for t in range(len(items) + 2 * lag):
+        for late, stage in ((0, arrived), (lag, joined), (2 * lag, complete)):
+            if 0 <= t - late < len(items):
+                stage(*items[t - late])
+    for k in range(count):
+        own(k).wait()
+        for step in range(1, depth):
+            outward(k, step).wait_send()
+        for shard in range(depth):
+            across(k, shard).wait_send()
+            across(k, shard).wait_recv()
+
+            @pl.when(shard != z)
+            def _():
+                joins(k, shard, 0).wait_send()
+                joins(k, shard, 1).wait_send()
+
+
+def gather_shards(arrays, ways):
+    count, depth = len(arrays), ways // 2
+    return pl.pallas_call(
+        functools.partial(gather_kernel, depth, count),
+        out_shape=[jax.ShapeDtypeStruct((ways,) + a.shape, a.dtype) for a in arrays],
+        in_specs=[pl.BlockSpec(memory_space=pl.ANY)] * count,
+        out_specs=[pl.BlockSpec(memory_space=pltpu.VMEM)] * count,
+        scratch_shapes=[pltpu.SemaphoreType.DMA((count,))]
+        + [pltpu.SemaphoreType.DMA((count, depth))] * 8,
+        compiler_params=pltpu.CompilerParams(
+            collective_id=1, has_side_effects=True, vmem_limit_bytes=VMEM_BYTES
+        ),
+    )(*[a[None] for a in arrays])
 
 
 def reduce_kernel(depth, count, *refs):
@@ -218,23 +234,22 @@
         device = [{"cp": 1 - x}, {"rep": 1 - y}, {"cp": 1 - x, "rep": 1 - y}][which]
         return remote(place, place, send4.at[k, which], recv4.at[k, which], device)
 
-    for k in range(count):
-        for j in range(depth):
-            copy0(k, j).start()
-    for k in range(count):
+    def over_cores(k):
         for j in range(depth):
             copy0(k, j).wait_recv()
             total = parts[k][2 * j + core].astype(f32) + first[k][j].astype(f32)
             held[k][j] = total.astype(held[k].dtype)
             copy1(k, j).start()
-    for k in range(count):
+
+    def over_first_axis(k):
         for j in range(depth):
-            own1, own2, _, _ = axes(j)
+            own1, _, _, _ = axes(j)
             copy1(k, j).wait_recv()
             half = part_of(held[k], j, own1, 2)
             half[...] = (half[...].astype(f32) + second[k][j].astype(f32)).astype(half.dtype)
             copy2(k, j).start()
-    for k in range(count):
+
+    def over_second_axis(k):
         for j in range(depth):
             own1, own2, _, _ = axes(j)
             copy2(k, j).wait_recv()
@@ -243,7 +258,8 @@
             quarter[k][j] = total.astype(quarter[k].dtype)
         for step in range(1, depth):
             copy3(k, step).start()
-    for k in range(count):
+
+    def over_z(k):
         total = quarter[k][z].astype(f32)
         for step in range(1, depth):
             copy3(k, step).wait_recv()
@@ -252,10 +268,20 @@
         place[...] = total.astype(place.dtype)
         for which in range(3):
             copy4(k, which).start()
-    for k in range(count):
+
+    def finish(k):
         for which in range(3):
             copy4(k, which).wait_recv()
         outs[k][...] = joined[k][0].astype(f32)
+
+    for k in range(count):
+        for j in range(depth):
+            copy0(k, j).start()
+    stages = (over_cores, over_first_axis, over_second_axis, over_z, finish)
+    for t in range(count + len(stages) - 1):
+        for late, stage in enumerate(stages):
+            if 0 <= t - late < count:
+                stage(t - late)
     for k in range(count):
         for j in range(depth):
             copy0(k, j).wait_send()
@@ -424,14 +450,20 @@
     row_span = residual.shape[0]
     query_columns = QUERY_HEADS * HEAD_SIZE
     key_columns = KEY_VALUE_HEADS * HEAD_SIZE
-    gains = jnp.zeros((16, 128), jnp.bfloat16)
-    gains = gains.at[0, : attn_gain.shape[0]].set(attn_gain).at[1, : mlp_gain.shape[0]].set(mlp_gain)
-    gathered = gather_shards([w_qkv, w_out, gains, w_gate, w_up, w_down], ways)
-    qkv_full, out_full, gate_full, up_full, down_full = [
-        gathered[i].reshape(-1, gathered[i].shape[-1]) for i in (0, 1, 3, 4, 5)
+    shard = attn_gain.shape[0]
+    gains = jnp.zeros((16, 512), jnp.bfloat16)
+    gains = gains.at[0, :shard].set(attn_gain).at[1, :shard].set(mlp_gain)
+    own_weights = [jnp.concatenate([w_qkv, w_out], axis=1), gains, w_gate, w_up, w_down]
+    if copies == (2, 2):
+        gathered = gather_shards(own_weights, ways)
+    else:
+        gathered = [lax.all_gather(w, "fsdp") for w in own_weights]
+    both_full, gate_full, up_full, down_full = [
+        gathered[i].reshape(-1, gathered[i].shape[-1]) for i in (0, 2, 3, 4)
     ]
-    gain_a = gathered[2][:, 0, : attn_gain.shape[0]].reshape(-1)
-    gain_m = gathered[2][:, 1, : mlp_gain.shape[0]].reshape(-1)
+    qkv_full, out_full = both_full[:, : w_qkv.shape[1]], both_full[:, w_qkv.shape[1] :]
+    gain_a = gathered[1][:, 0, :shard].reshape(-1)
+    gain_m = gathered[1][:, 1, :shard].reshape(-1)
     whole_ids = both_halves(segment_ids, 1)[0]
     every_length = whole_ids.shape[0]
     offset = lax.axis_index("cp") * row_span
@@ -519,7 +551,6 @@
     input_grad = d_mid + d_norm1
     if copies == (2, 2):
         bf16 = jnp.bfloat16
-        shard = attn_gain.shape[0]
         gain_grads = jnp.stack(
             [attn_gain_grad.reshape(ways, shard), mlp_gain_grad.reshape(ways, shard)], axis=1
         )
@@ -529,7 +560,7 @@
             g.astype(bf16).reshape(ways, -1, g.shape[-1])
             for g in (gate_grad, up_grad, down_grad, both)
         ]
-        gate_s, up_s, down_s, both_s, gain_s = reduce_shards(stacked + [gain_grads])
+        gain_s, gate_s, up_s, down_s, both_s = reduce_shards([gain_grads] + stacked)
         qkv_s, out_s = both_s[:, : w_qkv.shape[1]], both_s[:, w_qkv.shape[1] :]
         gain_a_s, gain_m_s = gain_s[0, :shard], gain_s[1, :shard]
     else:

time: 214 us -> 191 us (0.89)
  Pallas kernels: 125 us -> 104 us
  local copies, waits for them, and re-layouts: 20.4 us -> 17.4 us
  other arithmetic: 12 us -> 14.2 us
    pallas_call x1, Pallas kernels: 69 us -> 47.3 us  [gather_shards(): pl.pallas_call(functools.partial(gather_kernel, depth, count), out_shape=...]
    unnamed x55 -> x51, local copies, waits for them, and re-layouts: 9.58 us -> 7.59 us
  transfers between devices with their start and end apart: 3 -> 3, of which waited for: 2 -> 2; matrix products, arithmetic and copies ran while one was open for 8% -> 8% of each run, Pallas kernels for 32% -> 25%
where the time goes in v2:
time: 191 us; the launch traced here: 190 us
  Pallas kernels  104 us (54%)
  matrix products  40.2 us (21%)
  local copies, waits for them, and re-layouts  17.4 us (9%)
  other arithmetic  14.2 us (7%)
  waiting for transfers between devices  7.85 us (4%)
  starting transfers between devices  5.62 us (3%)
    pallas_call x1, Pallas kernels, reduce_shards(): pl.pallas_call(functools.partial(reduce_kernel, depth, count), out_shape=...  56.9 us
    pallas_call x1, Pallas kernels, gather_shards(): pl.pallas_call(functools.partial(gather_kernel, depth, count), out_shape=...  47.3 us
    dot_general x5, matrix products, transposed_times(): lax.dot_general(left, right, (((0,), (0,)), ((), ())), preferred_element_...  10.6 us
    dot_general x5, matrix products, times_transposed(): lax.dot_general(left, right, (((1,), (1,)), ((), ())), preferred_element_...  8.38 us
    ppermute x3, waiting for transfers between devices, swap_halves(): return lax.ppermute(value, 'cp', [(0, 1), (1, 0)])  7.85 us
    unnamed x51, local copies, waits for them, and re-layouts  7.59 us
    ppermute x3, starting transfers between devices, swap_halves(): return lax.ppermute(value, 'cp', [(0, 1), (1, 0)])  5.62 us
    dot_general x1, matrix products, attend_back(): jnp.einsum('nkgd,mkd->kgnm', grouped_gradient, values_three_axis, preferr...  3.96 us
  transfers between devices with their start and end apart: 3, of which 2 were waited for; matrix products, arithmetic and copies ran while one was open for 8% of the time, Pallas kernels for 25%

profile of v2, /device:TPU:0, one launch (start us, length us, event | category | flops | bytes accessed | tf_op | source)
XLA Modules:
  0.0 190.5 jit_solution(12689736643646348158)
XLA Ops:
  0.6 3.0 %collective-permute-start = (s32[1,384]{1,0:T(1,128)}, s32[1,384]{1,0:T(1,128)S(1)}, u32[]{:S(2)}, u32[]{:S(2)}) collective-permute-start(s32[1,384]{1,0:T(1,128)} %param.15), channel_id=1, source_target_pairs={{0,1},{1,0},{2,3},{3,2},{4,5},{5,4},{6,7},{7,6},{8,9},{9,8},{10,11... | collective-permute-start | bytes 4616 | tf_op jit(solution)/shard_map/ppermute | solution.py:435
  9.0 47.3 %shard_map.169 = (bf16[8,72,1536]{2,1,0:T(8,128)(2,1)S(1)}, bf16[8,16,512]{2,1,0:T(8,128)(2,1)S(1)}, bf16[8,72,1536]{2,1,0:T(8,128)(2,1)}, bf16[8,72,1536]{2,1,0:T(8,128)(2,1)}, bf16[8,192,576]{2,1,0:T(8,128)(2,1)}) custom-call(bf16[1,72,1536]{2,1,0:T(8,128)(2,1)S(1)} %maximum_bitcast_fusion.refs_0_, bf16[1,16,512]{2,1,0:T(8,128)(2,1)S(1)} %scatter.9.refs_1_, ...), custom_call_target="tpu_custom_call" | custom-call | tf_op jit(solution)/shard_map/pallas_call | solution.py:146
  57.6 2.0 %fusion.22 = f32[384,960]{0,1:T(8,128)S(1)} fusion(bf16[576,1536]{1,0:T(8,128)(2,1)S(1)} %bitcast.135, bf16[1,384,576]{1,2,0:T(8,128)(2,1)} %param.14, f32[576]{0:T(1024)S(1)} %reshape.396, f32[384]{0:T(512)S(1)} %add_rsqrt_fusion.1), kind=kOutput, calls=%fused_computation.51 | convolution fusion | flops 425558016 | bytes 3102720 | tf_op jit(solution)/shard_map/dot_general | solution.py:481
  64.1 1.4 collective-permute-start.1
  66.2 7.2 %collective-permute-done.1 = bf16[384,384]{0,1:T(8,128)(2,1)S(1)} collective-permute-done((bf16[384,384]{0,1:T(8,128)(2,1)S(1)}, bf16[384,384]{0,1:T(8,128)(2,1)S(1)}, u32[]{:S(2)}, u32[]{:S(2)}) %collective-permute-start.1) | collective-permute-done | bytes 294944 | tf_op jit(solution)/shard_map/ppermute | solution.py:435
  73.6 1.8 fusion.4
  75.4 2.2 %fusion.2 = f32[3,3,384]{2,1,0:T(4,128)S(1)} fusion(f32[3,768,384,3]{2,1,3,0:T(8,128)S(1)} %get-tuple-element.87, f32[3,3,384]{2,1,0:T(4,128)S(1)} %get-tuple-element.86, pred[384,768]{0,1:T(8,128)(4,1)S(1)} %fusion.19), kind=kLoop, calls=%fused_computation.7 | loop fusion | flops 10613376 | bytes 10939392 | tf_op jit(solution)/shard_map/reduce_sum | solution.py:391
  77.6 3.0 %fusion.15 = bf16[3,64,3,384]{3,1,2,0:T(8,128)(2,1)S(1)} fusion(bf16[768,3,64,1]{0,2,3,1:T(8,128)(2,1)S(1)} %bitcast.167, f32[3,768,384,3]{2,1,3,0:T(8,128)S(1)} %get-tuple-element.87, f32[3,3,384]{2,1,0:T(4,128)S(1)} %fusion.2, f32[3,3,384]{2,1,0:T(4,128)S(1)} %get-tuple-element.86, pred[384,768]{0,1:T(8,128)(4,1)S(1)} %fusion.19), kind=kOutput, calls=%fused_computation.42 | convolution fusion | flops 353230848 | bytes 11676672 | tf_op jit(solution)/shard_map/kgnm,mkd->nkgd/dot_general | solution.py:394
  85.2 3.1 %multiply_convert_fusion = (bf16[384,1536]{1,0:T(8,128)(2,1)S(1)}, bf16[384,1536]{1,0:T(8,128)(2,1)S(1)}, bf16[384,1536]{1,0:T(8,128)(2,1)}) fusion(f32[384,1536]{1,0:T(8,128)S(1)} %fusion.63, f32[384,1536]{1,0:T(8,128)S(1)} %fusion.64, bf16[1536,576]{1,0:T(8,128)(2,1)S(1)} %bitcast.172, bf16[1,384,576]{1,2,0:T(8,128)(2,1)S(1)} %copy-done.14), kind=kOutput, calls=%fused_computation.17 | convolution fusion | flops 688324608 | bytes 10469376 | tf_op jit(solution)/shard_map/dot_general | solution.py:349
  89.4 1.3 multiply_reduce_fusion
  91.8 2.7 %fusion.5 = f32[3,64,768,1]{2,1,3,0:T(8,128)S(1)} fusion(bf16[384,3,3,64]{0,3,2,1:T(8,128)(2,1)S(1)} %bitcast.154, f32[3,768,384,3]{2,1,3,0:T(8,128)S(1)} %get-tuple-element.87, f32[3,3,384]{2,1,0:T(4,128)S(1)} %log_add_fusion, pred[384,768]{0,1:T(8,128)(4,1)S(1)} %fusion.19), kind=kOutput, calls=%fused_computation.10 | convolution fusion | flops 350355456 | bytes 11957760 | tf_op jit(solution)/shard_map/kgnm,nkgd->mkd/dot_general | solution.py:409
  94.5 4.0 %fusion.1 = bf16[3,3,384,768]{2,3,1,0:T(8,128)(2,1)S(1)} fusion(f32[3,768,384,3]{2,1,3,0:T(8,128)S(1)} %get-tuple-element.87, f32[3,3,384]{2,1,0:T(4,128)S(1)} %bitcast.169, f32[3,3,384]{2,1,0:T(4,128)S(1)} %log_add_fusion, pred[384,768]{0,1:T(8,128)(4,1)S(1)} %fusion.19, bf16[768,3,64,1]{0,2,3,1:T(8,128)(2,1)S(1)} %bitcast.168, ...), kind=kOutput, calls=%fused_computation.2 | convolution fusion | flops 355663872 | bytes 16985088 | tf_op jit(solution)/shard_map/nkgd,mkd->kgnm/dot_general | solution.py:412
  99.4 1.7 fusion.17
  101.1 1.5 convolution_convert_fusion.4
  102.6 2.3 %convolution_convert_fusion.1 = bf16[576,1536]{1,0:T(8,128)(2,1)} fusion(bf16[384,576]{0,1:T(8,128)(2,1)S(1)} %multiply_convert_fusion.3, bf16[384,1536]{1,0:T(8,128)(2,1)S(1)} %get-tuple-element.59), kind=kOutput, calls=%fused_computation.14 | convolution fusion | flops 680361984 | bytes 3391488 | tf_op jit(solution)/shard_map/dot_general | solution.py:355
  104.9 2.3 %convolution_convert_fusion = bf16[1536,576]{0,1:T(8,128)(2,1)} fusion(bf16[384,1536]{1,0:T(8,128)(2,1)S(1)} %copy-done.22, bf16[1,384,576]{1,2,0:T(8,128)(2,1)S(1)} %copy-done.14), kind=kOutput, calls=%fused_computation.13 | convolution fusion | flops 680361984 | bytes 3391488 | tf_op jit(solution)/shard_map/dot_general | solution.py:355
  107.2 1.9 fusion.18
  110.8 1.3 collective-permute-start.2
  112.2 3.9 %copy.40 = bf16[1536,576]{1,0:T(8,128)(2,1)} copy(bf16[1536,576]{0,1:T(8,128)(2,1)} %convolution_convert_fusion) | data formatting | bytes 3538944 | tf_op jit(solution)/shard_map/convert_element_type | solution.py:560
  116.3 2.6 %convolution_convert_fusion.2 = bf16[576,1536]{1,0:T(8,128)(2,1)S(1)} fusion(bf16[384,576]{0,1:T(8,128)(2,1)} %copy-done.15, bf16[384,1536]{1,0:T(8,128)(2,1)} %copy-done.23), kind=kOutput, calls=%fused_computation.15 | convolution fusion | flops 680361984 | bytes 3391488 | tf_op jit(solution)/shard_map/dot_general | solution.py:355
  120.6 1.9 convolution_convert_fusion.3
  122.5 2.3 %fusion.30 = (bf16[576]{0:T(1024)(128)(2,1)S(1)}, f32[384]{0:T(512)}, f32[384,576]{0,1:T(8,128)}) fusion(bf16[1,384,576]{1,2,0:T(8,128)(2,1)S(1)} %copy-done.10, f32[384]{0:T(512)S(1)} %add_rsqrt_fusion.1, f32[576]{0:T(1024)S(1)} %reshape.396, bf16[384,384]{0,1:T(8,128)(2,1)S(1)} %fusion.38, bf16[384,576]{0,1:T(8,128)(2,1)S(1)} %bitcast.166, ...), kind=kOutput, calls=%fused_computation.59 | convolution fusion | flops 427695168 | bytes 3252864 | tf_op jit(solution)/shard_map/dot_general | solution.py:349
  124.9 3.1 %pad_maximum_fusion = bf16[576,1536]{1,0:T(8,128)(2,1)} fusion(bf16[576,576]{1,0:T(8,128)(2,1)} %convolution_convert_fusion.4, bf16[576,960]{1,0:T(8,128)(2,1)} %convolution_convert_fusion.3), kind=kLoop, calls=%fused_computation.23 | loop fusion | flops 3538944 | bytes 3538944 | tf_op jit(solution)/shard_map/concatenate | solution.py:558
  128.1 56.9 %shard_map.170 = (f32[16,512]{1,0:T(8,128)S(1)}, f32[72,1536]{1,0:T(8,128)S(1)}, f32[72,1536]{1,0:T(8,128)S(1)}, f32[192,576]{1,0:T(8,128)S(1)}, f32[72,1536]{1,0:T(8,128)S(1)}) custom-call(bf16[8,16,512]{2,1,0:T(8,128)(2,1)S(1)} %fusion.50.refs_0_, bf16[8,72,1536]{2,1,0:T(8,128)(2,1)S(1)} %bitcast.134, bf16[8,72,1536]{2,1,0:T(8,128)(2,1)} %bitcast.150, ...), custom_call_target="tpu_custom_call" | custom-call | tf_op jit(solution)/shard_map/pallas_call | solution.py:312
  (106 shorter events, 29.0 us)
Async XLA Ops:
  0.6 61.5 %collective-permute-start = (s32[1,384]{1,0:T(1,128)}, s32[1,384]{1,0:T(1,128)S(1)}, u32[]{:S(2)}, u32[]{:S(2)}) collective-permute-start(s32[1,384]{1,0:T(1,128)} %param.15), channel_id=1, source_target_pairs={{0,1},{1,0},{2,3},{3,2},{4,5},{5,4},{6,7},{7,6},{8,9},{9,8},{10,11... | collective-permute-start | bytes 4616 | tf_op jit(solution)/shard_map/ppermute | solution.py:435
  6.2 0.9 copy-start
  57.6 4.6 %copy-start.17 = (s32[1,384]{1,0:T(1,128)S(1)}, s32[1,384]{1,0:T(1,128)}, u32[]{:S(2)}) copy-start(s32[1,384]{1,0:T(1,128)} %param.15) | copy-start | bytes 4612
  59.6 1.3 copy-start.12
  64.1 9.3 %collective-permute-start.1 = (bf16[384,384]{0,1:T(8,128)(2,1)S(1)}, bf16[384,384]{0,1:T(8,128)(2,1)S(1)}, u32[]{:S(2)}, u32[]{:S(2)}) collective-permute-start(bf16[384,384]{0,1:T(8,128)(2,1)S(1)} %pad_maximum_fusion.8), channel_id=1, source_target_pairs={{0,1},{1,0},{2,3},{3,2},{4,5},{5,4},{6,7},{7,6},{8,9},{9,8},{10,11... | collective-permute-start | bytes 884744 | tf_op jit(solution)/shard_map/ppermute | solution.py:435
  77.5 3.1 %copy-start.9 = (bf16[1,384,576]{1,2,0:T(8,128)(2,1)S(1)}, bf16[1,384,576]{1,2,0:T(8,128)(2,1)}, u32[]{:S(2)}) copy-start(bf16[1,384,576]{1,2,0:T(8,128)(2,1)} %param.14) | copy-start | bytes 1327108
  80.6 1.5 copy-start.20
  81.8 20.7 %copy-start.15 = (bf16[384,576]{0,1:T(8,128)(2,1)}, bf16[384,576]{0,1:T(8,128)(2,1)S(1)}, u32[]{:S(2)}) copy-start(bf16[384,576]{0,1:T(8,128)(2,1)S(1)} %multiply_convert_fusion.3) | copy-start | bytes 1327108
  82.1 1.5 copy-start.21
  83.5 1.1 copy-start.14
  83.6 1.7 copy-start.18
  88.3 1.1 copy-start.23
  91.0 10.1 %copy-start.3 = (f32[384,576]{0,1:T(8,128)}, f32[384,576]{0,1:T(8,128)S(1)}, u32[]{:S(2)}) copy-start(f32[384,576]{0,1:T(8,128)S(1)} %multiply_add_fusion) | copy-start | bytes 2654212
  94.5 14.8 %copy-start.7 = (f32[3,64,768,1]{2,1,3,0:T(8,128)}, f32[3,64,768,1]{2,1,3,0:T(8,128)S(1)}, u32[]{:S(2)}) copy-start(f32[3,64,768,1]{2,1,3,0:T(8,128)S(1)} %fusion.5) | copy-start | bytes 1769476
  102.6 2.3 %copy-start.22 = (bf16[384,1536]{1,0:T(8,128)(2,1)S(1)}, bf16[384,1536]{1,0:T(8,128)(2,1)}, u32[]{:S(2)}) copy-start(bf16[384,1536]{1,0:T(8,128)(2,1)} %get-tuple-element.61) | copy-start | bytes 3538948
  104.9 2.3 %copy-start.19 = (bf16[8,192,576]{2,1,0:T(8,128)(2,1)S(1)}, bf16[8,192,576]{2,1,0:T(8,128)(2,1)}, u32[]{:S(2)}) copy-start(bf16[8,192,576]{2,1,0:T(8,128)(2,1)} %get-tuple-element.47) | copy-start | bytes 5308420
  110.8 8.8 %collective-permute-start.2 = (bf16[384,384]{0,1:T(8,128)(2,1)}, bf16[384,384]{0,1:T(8,128)(2,1)}, u32[]{:S(2)}, u32[]{:S(2)}) collective-permute-start(bf16[384,384]{0,1:T(8,128)(2,1)} %fusion.35), channel_id=1, source_target_pairs={{0,1},{1,0},{2,3},{3,2},{4,5},{5,4},{6,7},{7,6},{8,9},{9,8},{10,11... | collective-permute-start | bytes 884744 | tf_op jit(solution)/shard_map/ppermute | solution.py:435
  116.2 3.3 %copy-start.6 = (f32[768,3,64]{0,2,1:T(8,128)S(1)}, f32[768,3,64]{0,2,1:T(8,128)}, u32[]{:S(2)}) copy-start(f32[768,3,64]{0,2,1:T(8,128)} %copy-done.5) | copy-start | bytes 1769476
  116.3 3.3 %copy-start.8 = (f32[3,64,768,1]{2,1,3,0:T(8,128)S(1)}, f32[3,64,768,1]{2,1,3,0:T(8,128)}, u32[]{:S(2)}) copy-start(f32[3,64,768,1]{2,1,3,0:T(8,128)} %copy-done.7) | copy-start | bytes 1769476
  116.3 4.4 %copy-start.10 = (bf16[1,384,576]{1,2,0:T(8,128)(2,1)S(1)}, bf16[1,384,576]{1,2,0:T(8,128)(2,1)}, u32[]{:S(2)}) copy-start(bf16[1,384,576]{1,2,0:T(8,128)(2,1)} %param.14) | copy-start | bytes 1327108
  128.0 59.0 %copy-start.16 = (f32[384]{0:T(512)S(1)}, f32[384]{0:T(512)}, u32[]{:S(2)}) copy-start(f32[384]{0:T(512)} %get-tuple-element.56) | copy-start | bytes 4612
  128.0 59.0 %copy-start.4 = (f32[384,576]{0,1:T(8,128)S(1)}, f32[384,576]{0,1:T(8,128)}, u32[]{:S(2)}) copy-start(f32[384,576]{0,1:T(8,128)} %copy-done.3) | copy-start | bytes 2654212
  128.0 59.0 %copy-start.11 = (bf16[1,384,576]{1,2,0:T(8,128)(2,1)S(1)}, bf16[1,384,576]{1,2,0:T(8,128)(2,1)}, u32[]{:S(2)}) copy-start(bf16[1,384,576]{1,2,0:T(8,128)(2,1)} %param.14) | copy-start | bytes 1327108
  128.1 59.0 %copy-start.13 = (f32[384,576]{0,1:T(8,128)S(1)}, f32[384,576]{0,1:T(8,128)}, u32[]{:S(2)}) copy-start(f32[384,576]{0,1:T(8,128)} %get-tuple-element.91) | copy-start | bytes 2654212
  (3 other events, 2.7 us)

commit v3 on v2

--- a/solution.py
+++ b/solution.py
@@ -157,8 +157,9 @@
 
 
 def reduce_kernel(depth, count, *refs):
-    parts, outs = refs[:count], refs[count : 2 * count]
-    rest = refs[2 * count :]
+    gains, factors, rest = refs[0], refs[1 : 2 * count - 1], refs[2 * count - 1 :]
+    outs, products, rest = rest[:count], rest[count : 2 * count - 1], rest[2 * count - 1 :]
+    parts = (gains,) + tuple(products)
     first, second, third, fourth, held, quarter, joined = [
         rest[i * count : (i + 1) * count] for i in range(7)
     ]
@@ -233,6 +234,40 @@
         place = part_of(joined[k], 0, mine, 4)
         device = [{"cp": 1 - x}, {"rep": 1 - y}, {"cp": 1 - x, "rep": 1 - y}][which]
         return remote(place, place, send4.at[k, which], recv4.at[k, which], device)
+
+    def multiply(k):
+        if k > 0:
+            left, right = factors[2 * k - 2], factors[2 * k - 1]
+            ways, rows, columns = parts[k].shape
+            contract = (((0,), (0,)), ((), ()))
+            if columns % 512 == 0:
+
+                def some_columns(n, carry):
+                    span = pl.ds(pl.multiple_of(n * 512, 512), 512)
+                    product = lax.dot_general(
+                        left[...], right[:, span], contract, preferred_element_type=f32
+                    )
+                    for i in range(ways):
+                        block = product[i * rows : (i + 1) * rows]
+                        parts[k][i, :, span] = block.astype(parts[k].dtype)
+                    return carry
+
+                lax.fori_loop(0, columns // 512, some_columns, 0)
+            else:
+
+                def some_rows(n, carry):
+                    span = pl.ds(pl.multiple_of(n * 2 * rows, 2 * rows), 2 * rows)
+                    product = lax.dot_general(
+                        left[:, span], right[...], contract, preferred_element_type=f32
+                    )
+                    for i in range(2):
+                        block = product[i * rows : (i + 1) * rows]
+                        parts[k][2 * n + i] = block.astype(parts[k].dtype)
+                    return carry
+
+                lax.fori_loop(0, ways // 2, some_rows, 0)
+        for j in range(depth):
+            copy0(k, j).start()
 
     def over_cores(k):
         for j in range(depth):
@@ -274,10 +309,7 @@
             copy4(k, which).wait_recv()
         outs[k][...] = joined[k][0].astype(f32)
 
-    for k in range(count):
-        for j in range(depth):
-            copy0(k, j).start()
-    stages = (over_cores, over_first_axis, over_second_axis, over_z, finish)
+    stages = (multiply, over_cores, over_first_axis, over_second_axis, over_z, finish)
     for t in range(count + len(stages) - 1):
         for late, stage in enumerate(stages):
             if 0 <= t - late < count:
@@ -293,10 +325,15 @@
             copy4(k, which).wait_send()
 
 
-def reduce_shards(arrays):
-    count, ways = len(arrays), arrays[0].shape[0]
-    depth = ways // 2
-    kind = arrays[0].dtype
+def reduce_shards(gains, factors):
+    ways = gains.shape[0]
+    depth, kind = ways // 2, gains.dtype
+    arrays = [gains] + [
+        jax.ShapeDtypeStruct((ways, left.shape[1] // ways, right.shape[1]), kind)
+        for left, right in factors
+    ]
+    count = len(arrays)
+    operands = [gains] + [f for pair in factors for f in pair]
     wholes = [(depth,) + a.shape[1:] for a in arrays]
     halves, quarters = [], []
     for a in arrays:
@@ -304,7 +341,7 @@
         by_columns = columns % (4 * 128) == 0
         halves.append((depth, rows, columns // 2) if by_columns else (depth, rows // 2, columns))
         quarters.append((depth, rows, columns // 4) if by_columns else (depth, rows // 4, columns))
-    buffers = []
+    buffers = [pltpu.VMEM(a.shape, kind) for a in arrays[1:]]
     for shapes in (wholes, halves, quarters, quarters, wholes, quarters):
         buffers += [pltpu.VMEM(s, kind) for s in shapes]
     buffers += [pltpu.VMEM((1,) + a.shape[1:], kind) for a in arrays]
@@ -312,13 +349,13 @@
     return pl.pallas_call(
         functools.partial(reduce_kernel, depth, count),
         out_shape=[jax.ShapeDtypeStruct(a.shape[1:], jnp.float32) for a in arrays],
-        in_specs=[pl.BlockSpec(memory_space=pltpu.VMEM)] * count,
+        in_specs=[pl.BlockSpec(memory_space=pltpu.VMEM)] * len(operands),
         out_specs=[pl.BlockSpec(memory_space=pltpu.VMEM)] * count,
         scratch_shapes=buffers + sems,
         compiler_params=pltpu.CompilerParams(
             collective_id=2, has_side_effects=True, vmem_limit_bytes=VMEM_BYTES
         ),
-    )(*arrays)
+    )(*operands)
 
 
 def rope_tables(positions):
@@ -478,16 +515,17 @@
     query_cosine, query_sine = rope_tables(query_positions)
     k_cos, k_sin = rope_tables(key_positions)
     normed1, inv_rms1, xn = norm_forward(residual, gain_a)
-    output_projection = jnp.dot(xn, qkv_full, preferred_element_type=jnp.float32)
+    key_projection = jnp.dot(xn, qkv_full[:, query_columns:], preferred_element_type=jnp.float32)
+    query_projection = jnp.dot(xn, qkv_full[:, :query_columns], preferred_element_type=jnp.float32)
     query_rows = apply_rotation(
-        output_projection[:, :query_columns].reshape(row_span, QUERY_HEADS, HEAD_SIZE),
+        query_projection.reshape(row_span, QUERY_HEADS, HEAD_SIZE),
         query_cosine,
         query_sine,
         1.0,
     ).astype(jnp.bfloat16)
     keys_local = (
         apply_rotation(
-            output_projection[:, query_columns : query_columns + key_columns].reshape(
+            key_projection[:, :key_columns].reshape(
                 row_span, KEY_VALUE_HEADS, HEAD_SIZE
             ),
             query_cosine,
@@ -497,8 +535,15 @@
         .astype(jnp.bfloat16)
         .reshape(row_span, key_columns)
     )
-    values_local = output_projection[:, query_columns + key_columns :].astype(jnp.bfloat16)
-    every_pair = both_halves(jnp.concatenate([keys_local, values_local], axis=1), 0)
+    values_local = key_projection[:, key_columns:].astype(jnp.bfloat16)
+    pair_local = jnp.concatenate([keys_local, values_local], axis=1)
+    pair_other = swap_halves(pair_local)
+    d_act = times_transposed(out_cotangent[0], down_full)
+    pair_other, query_rows, d_act = lax.optimization_barrier((pair_other, query_rows, d_act))
+    first = lax.axis_index("cp") == 0
+    every_pair = jnp.concatenate(
+        [jnp.where(first, pair_local, pair_other), jnp.where(first, pair_other, pair_local)], axis=0
+    )
     every_key, every_value = every_pair[:, :key_columns], every_pair[:, key_columns:]
     keys_three_axis = every_key.reshape(every_length, KEY_VALUE_HEADS, HEAD_SIZE)
     values_three_axis = every_value.reshape(every_length, KEY_VALUE_HEADS, HEAD_SIZE)
@@ -514,7 +559,6 @@
         jnp.bfloat16
     )
     cotangent = out_cotangent[0]
-    d_act = times_transposed(cotangent, down_full)
     down_grad = transposed_times(act, cotangent)
     d_gate = (d_act * up_val * sigma * (1.0 + gate * (1.0 - sigma))).astype(jnp.bfloat16)
     d_up = (d_act * silu_gate).astype(jnp.bfloat16)
@@ -555,12 +599,19 @@
             [attn_gain_grad.reshape(ways, shard), mlp_gain_grad.reshape(ways, shard)], axis=1
         )
         gain_grads = jnp.pad(gain_grads, ((0, 0), (0, 14), (0, 512 - shard))).astype(bf16)
-        both = jnp.concatenate([qkv_grad.astype(bf16), out_grad.astype(bf16)], axis=1)
-        stacked = [
-            g.astype(bf16).reshape(ways, -1, g.shape[-1])
-            for g in (gate_grad, up_grad, down_grad, both)
-        ]
-        gain_s, gate_s, up_s, down_s, both_s = reduce_shards([gain_grads] + stacked)
+        width = d_mid_b.shape[1]
+        both = (
+            jnp.concatenate([xn, attn_mix], axis=0),
+            jnp.concatenate(
+                [
+                    jnp.pad(d_proj, ((0, 0), (0, width))),
+                    jnp.pad(d_mid_b, ((0, 0), (d_proj.shape[1], 0))),
+                ],
+                axis=0,
+            ),
+        )
+        factors = [(hidden_n, d_gate), (hidden_n, d_up), (act, cotangent), both]
+        gain_s, gate_s, up_s, down_s, both_s = reduce_shards(gain_grads, factors)
         qkv_s, out_s = both_s[:, : w_qkv.shape[1]], both_s[:, w_qkv.shape[1] :]
         gain_a_s, gain_m_s = gain_s[0, :shard], gain_s[1, :shard]
     else:

time: 191 us -> 201 us (1.052)
  local copies, waits for them, and re-layouts: 17.4 us -> 25.9 us
  other arithmetic: 14.2 us -> 20.1 us
  matrix products: 40.2 us -> 36.3 us
  waiting for transfers between devices: 7.85 us -> 5.34 us
    dot_general x6 -> x2, matrix products: 12.5 us -> 4.22 us  [the longest x1 2.62 us: shards(): jnp.dot(xn, qkv_full[:, query_columns:], preferred_element_type=jnp.float32)]
    unnamed x51 -> x61, local copies, waits for them, and re-layouts: 7.59 us -> 13.1 us
    reshape x0 -> x3, local copies, waits for them, and re-layouts: none -> 4.57 us  [the longest x1 2.24 us: shards(): apply_rotation(d_keys, k_cos, k_sin, -1.0)]
    convert_element_type x0 -> x2, other arithmetic: none -> 3 us  [the longest x1 2.68 us: shards(): (d_act * up_val * sigma * (1.0 + gate * (1.0 - sigma))).astype(jnp.bfloat16)]
    ppermute x3, waiting for transfers between devices: 7.85 us -> 5.34 us  [swap_halves(): return lax.ppermute(value, 'cp', [(0, 1), (1, 0)])]
    dot_general x0 -> x2, local copies, waits for them, and re-layouts: none -> 2.39 us  [shards(): jnp.dot(xn, qkv_full[:, :query_columns], preferred_element_type=jnp.float32)]
    slice x3, local copies, waits for them, and re-layouts: 2.08 us -> 0.02 us  [the longest x1 0.02 us: shards(): values_local = key_projection[:, key_columns:].astype(jnp.bfloat16)]
  transfers between devices with their start and end apart: 3 -> 3, of which waited for: 2 -> 1; matrix products, arithmetic and copies ran while one was open for 8% -> 15% of each run, Pallas kernels for 25% -> 24%
where the time goes in v3:
time: 201 us; the launch traced here: 200 us
  Pallas kernels  105 us (52%)
  matrix products  36.3 us (18%)
  local copies, waits for them, and re-layouts  25.9 us (13%)
  other arithmetic  20.1 us (10%)
  starting transfers between devices  5.62 us (3%)
  waiting for transfers between devices  5.34 us (3%)
    pallas_call x1, Pallas kernels, reduce_shards(): pl.pallas_call(functools.partial(reduce_kernel, depth, count), out_shape=...  58 us
    pallas_call x1, Pallas kernels, gather_shards(): pl.pallas_call(functools.partial(gather_kernel, depth, count), out_shape=...  47.4 us
    unnamed x61, local copies, waits for them, and re-layouts  13.1 us
    dot_general x5, matrix products, times_transposed(): lax.dot_general(left, right, (((1,), (1,)), ((), ())), preferred_element_...  9.07 us
    ppermute x3, starting transfers between devices, swap_halves(): return lax.ppermute(value, 'cp', [(0, 1), (1, 0)])  5.62 us
    ppermute x3, waiting for transfers between devices, swap_halves(): return lax.ppermute(value, 'cp', [(0, 1), (1, 0)])  5.34 us
  transfers between devices with their start and end apart: 3, of which 1 were waited for; matrix products, arithmetic and copies ran while one was open for 15% of the time, Pallas kernels for 24%

profile of v3, /device:TPU:0, one launch (start us, length us, event | category | flops | bytes accessed | tf_op | source)
XLA Modules:
  0.0 199.8 jit_solution(14749429405098934878)
XLA Ops:
  0.6 3.0 %collective-permute-start = (s32[1,384]{1,0:T(1,128)}, s32[1,384]{1,0:T(1,128)S(1)}, u32[]{:S(2)}, u32[]{:S(2)}) collective-permute-start(s32[1,384]{1,0:T(1,128)} %param.15), channel_id=1, source_target_pairs={{0,1},{1,0},{2,3},{3,2},{4,5},{5,4},{6,7},{7,6},{8,9},{9,8},{10,11... | collective-permute-start | bytes 4616 | tf_op jit(solution)/shard_map/ppermute | solution.py:472
  9.0 47.4 %shard_map.169 = (bf16[8,72,1536]{2,1,0:T(8,128)(2,1)S(1)}, bf16[8,16,512]{2,1,0:T(8,128)(2,1)S(1)}, bf16[8,72,1536]{2,1,0:T(8,128)(2,1)}, bf16[8,72,1536]{2,1,0:T(8,128)(2,1)}, bf16[8,192,576]{2,1,0:T(8,128)(2,1)}) custom-call(bf16[1,72,1536]{2,1,0:T(8,128)(2,1)S(1)} %maximum_bitcast_fusion.refs_0_, bf16[1,16,512]{2,1,0:T(8,128)(2,1)S(1)} %scatter.9.refs_1_, ...), custom_call_target="tpu_custom_call" | custom-call | tf_op jit(solution)/shard_map/pallas_call | solution.py:146
  56.5 1.6 copy.63
  60.1 2.6 %fusion.49 = f32[384,384]{0,1:T(8,128)} fusion(bf16[384,576]{1,0:T(8,128)(2,1)} %fusion.27, bf16[576,1536]{1,0:T(8,128)(2,1)S(1)} %bitcast.160), kind=kOutput, calls=%fused_computation.85 | convolution fusion | flops 169869312 | bytes 1474560 | tf_op jit(solution)/shard_map/dot_general | solution.py:518
  62.8 1.5 copy.64
  64.2 1.6 fusion.45
  65.8 4.2 %convolution_bitcast_fusion = f32[384,1536]{1,0:T(8,128)} fusion(bf16[1536,576]{1,0:T(8,128)(2,1)} %bitcast.174, bf16[1,384,576]{1,2,0:T(8,128)(2,1)} %param.23), kind=kOutput, calls=%fused_computation.17 | convolution fusion | flops 679477248 | bytes 4571136 | tf_op jit(solution)/shard_map/dot_general | solution.py:386
  77.0 5.3 %collective-permute-done.1 = bf16[384,384]{0,1:T(8,128)(2,1)S(1)} collective-permute-done((bf16[384,384]{0,1:T(8,128)(2,1)S(1)}, bf16[384,384]{0,1:T(8,128)(2,1)S(1)}, u32[]{:S(2)}, u32[]{:S(2)}) %collective-permute-start.1) | collective-permute-done | bytes 294944 | tf_op jit(solution)/shard_map/ppermute | solution.py:472
  82.5 1.8 fusion.4
  84.3 2.2 %fusion.2 = f32[3,3,384]{2,1,0:T(4,128)S(1)} fusion(f32[3,768,384,3]{2,1,3,0:T(8,128)S(1)} %get-tuple-element.120, f32[3,3,384]{2,1,0:T(4,128)S(1)} %get-tuple-element.119, pred[384,768]{0,1:T(8,128)(4,1)S(1)} %fusion.26), kind=kLoop, calls=%fused_computation.7 | loop fusion | flops 10613376 | bytes 10939392 | tf_op jit(solution)/shard_map/reduce_sum | solution.py:428
  86.4 3.2 %fusion.14 = bf16[3,64,3,384]{3,1,2,0:T(8,128)(2,1)S(1)} fusion(bf16[768,3,64,1]{0,2,3,1:T(8,128)(2,1)S(1)} %bitcast.188, f32[3,768,384,3]{2,1,3,0:T(8,128)S(1)} %get-tuple-element.120, f32[3,3,384]{2,1,0:T(4,128)S(1)} %fusion.2, f32[3,3,384]{2,1,0:T(4,128)S(1)} %get-tuple-element.119, pred[384,768]{0,1:T(8,128)(4,1)S(1)} %fusion.26), kind=kOutput, calls=%fused_computation.35 | convolution fusion | flops 353230848 | bytes 11676672 | tf_op jit(solution)/shard_map/kgnm,mkd->nkgd/dot_general | solution.py:431
  94.4 2.7 %multiply_convert_fusion.1 = (bf16[384,1536]{1,0:T(8,128)(2,1)S(1)}, bf16[384,1536]{1,0:T(8,128)(2,1)S(1)}, bf16[384,1536]{1,0:T(8,128)(2,1)}) fusion(f32[384,1536]{1,0:T(8,128)S(1)} %fusion.66, f32[384,1536]{1,0:T(8,128)S(1)} %copy-done.11, f32[384,1536]{1,0:T(8,128)S(1)} %fusion.67), kind=kLoop, calls=%fused_computation.20 | loop fusion | flops 8847360 | bytes 10616832 | tf_op jit(solution)/shard_map/convert_element_type | solution.py:563
  101.1 3.6 %fusion.5 = f32[3,64,768,1]{2,1,3,0:T(8,128)} fusion(bf16[384,3,3,64]{0,3,2,1:T(8,128)(2,1)S(1)} %bitcast.186, f32[3,768,384,3]{2,1,3,0:T(8,128)S(1)} %get-tuple-element.120, f32[3,3,384]{2,1,0:T(4,128)S(1)} %log_add_fusion, pred[384,768]{0,1:T(8,128)(4,1)S(1)} %fusion.26), kind=kOutput, calls=%fused_computation.10 | convolution fusion | flops 350355456 | bytes 11957760 | tf_op jit(solution)/shard_map/kgnm,nkgd->mkd/dot_general | solution.py:446
  104.7 4.0 %fusion.1 = bf16[3,3,384,768]{2,3,1,0:T(8,128)(2,1)S(1)} fusion(f32[3,768,384,3]{2,1,3,0:T(8,128)S(1)} %get-tuple-element.120, f32[3,3,384]{2,1,0:T(4,128)S(1)} %bitcast.190, f32[3,3,384]{2,1,0:T(4,128)S(1)} %log_add_fusion, pred[384,768]{0,1:T(8,128)(4,1)S(1)} %fusion.26, bf16[768,3,64,1]{0,2,3,1:T(8,128)(2,1)S(1)} %bitcast.189, ...), kind=kOutput, calls=%fused_computation.2 | convolution fusion | flops 355663872 | bytes 16985088 | tf_op jit(solution)/shard_map/nkgd,mkd->kgnm/dot_general | solution.py:449
  108.7 1.9 convolution_multiply_fusion
  110.6 1.6 fusion.16
  114.5 2.2 %copy.76 = f32[768,192]{1,0:T(8,128)} copy(f32[768,192]{0,1:T(8,128)} %bitcast.173) | data formatting | bytes 1179648 | tf_op jit(solution)/shard_map/reshape | solution.py:576
  116.8 1.8 fusion.40
  119.9 3.8 %fusion.23 = bf16[1,384,576]{2,1,0:T(8,128)(2,1)} fusion(f32[384,576]{1,0:T(8,128)S(1)} %copy-done.6, bf16[384,1536]{1,0:T(8,128)(2,1)} %get-tuple-element.94.refs_5_, bf16[1536,576]{1,0:T(8,128)(2,1)} %bitcast.175), kind=kOutput, calls=%fused_computation.47 | convolution fusion | flops 679919616 | bytes 4276224 | tf_op jit(solution)/shard_map/dot_general | solution.py:558
  123.9 2.0 %copy.83 = bf16[384,576]{1,0:T(8,128)(2,1)} copy(bf16[384,576]{0,1:T(8,128)(2,1)} %bitcast.178) | data formatting | bytes 884736 | tf_op jit(solution)/shard_map/convert_element_type | solution.py:434
  127.0 2.0 copy.84
  132.0 1.8 fusion.33
  133.8 1.7 fusion.11.refs_8_
  135.7 58.0 %shard_map.170 = (f32[16,512]{1,0:T(8,128)S(1)}, f32[72,1536]{1,0:T(8,128)S(1)}, f32[72,1536]{1,0:T(8,128)S(1)}, f32[192,576]{1,0:T(8,128)S(1)}, f32[72,1536]{1,0:T(8,128)S(1)}) custom-call(bf16[8,16,512]{2,1,0:T(8,128)(2,1)S(1)} %fusion.58.refs_0_, bf16[384,576]{1,0:T(8,128)(2,1)S(1)} %multiply_convert_fusion.3.refs_1_.refs_3_, ...), custom_call_target="tpu_custom_call" | custom-call | tf_op jit(solution)/shard_map/pallas_call | solution.py:349
  (122 shorter events, 37.2 us)
Async XLA Ops:
  0.6 70.8 %collective-permute-start = (s32[1,384]{1,0:T(1,128)}, s32[1,384]{1,0:T(1,128)S(1)}, u32[]{:S(2)}, u32[]{:S(2)}) collective-permute-start(s32[1,384]{1,0:T(1,128)} %param.15), channel_id=1, source_target_pairs={{0,1},{1,0},{2,3},{3,2},{4,5},{5,4},{6,7},{7,6},{8,9},{9,8},{10,11... | collective-permute-start | bytes 4616 | tf_op jit(solution)/shard_map/ppermute | solution.py:472
  56.3 43.9 %copy-start = (bf16[8,72,1536]{2,1,0:T(8,128)(2,1)}, bf16[8,72,1536]{2,1,0:T(8,128)(2,1)S(1)}, u32[]{:S(2)}) copy-start(bf16[8,72,1536]{2,1,0:T(8,128)(2,1)S(1)} %get-tuple-element.47) | copy-start | bytes 5308420
  58.0 73.9 %copy-start.8 = (bf16[1,384,576]{2,1,0:T(8,128)(2,1)}, bf16[1,384,576]{2,1,0:T(8,128)(2,1)S(1)}, u32[]{:S(2)}) copy-start(bf16[1,384,576]{2,1,0:T(8,128)(2,1)S(1)} %copy.63) | copy-start | bytes 1327108
  65.8 4.2 %copy-start.19 = (f32[384,384]{0,1:T(8,128)S(1)}, f32[384,384]{0,1:T(8,128)}, u32[]{:S(2)}) copy-start(f32[384,384]{0,1:T(8,128)} %fusion.49) | copy-start | bytes 1769476
  65.8 5.6 %copy-start.25 = (s32[1,384]{1,0:T(1,128)S(1)}, s32[1,384]{1,0:T(1,128)}, u32[]{:S(2)}) copy-start(s32[1,384]{1,0:T(1,128)} %param.15) | copy-start | bytes 4612
  65.8 7.0 %slice-start = ((f32[384,384]{0,1:T(8,128)}), f32[384,192]{0,1:T(8,128)S(1)}, s32[]{:S(2)}) async-start(f32[384,384]{0,1:T(8,128)} %fusion.49), calls=%async_computation | async-start | bytes 589824 | tf_op jit(solution)/shard_map/slice | solution.py:528
  73.0 9.3 %collective-permute-start.1 = (bf16[384,384]{0,1:T(8,128)(2,1)S(1)}, bf16[384,384]{0,1:T(8,128)(2,1)S(1)}, u32[]{:S(2)}, u32[]{:S(2)}) collective-permute-start(bf16[384,384]{0,1:T(8,128)(2,1)S(1)} %pad_maximum_fusion.6), channel_id=1, source_target_pairs={{0,1},{1,0},{2,3},{3,2},{4,5},{5,4},{6,7},{7,6},{8,9},{9,8},{10,11... | collective-permute-start | bytes 884744 | tf_op jit(solution)/shard_map/ppermute | solution.py:472
  89.6 11.3 %copy-start.20 = (bf16[3,64,3,384]{3,1,2,0:T(8,128)(2,1)}, bf16[3,64,3,384]{3,1,2,0:T(8,128)(2,1)S(1)}, u32[]{:S(2)}) copy-start(bf16[3,64,3,384]{3,1,2,0:T(8,128)(2,1)S(1)} %fusion.14) | copy-start | bytes 1327108
  89.7 1.6 copy-start.26
  90.6 9.3 %copy-start.5 = (f32[384,576]{1,0:T(8,128)}, f32[384,576]{1,0:T(8,128)S(1)}, u32[]{:S(2)}) copy-start(f32[384,576]{1,0:T(8,128)S(1)} %get-tuple-element.122) | copy-start | bytes 2654212
  92.8 1.7 copy-start.11
  100.2 4.5 %copy-start.16 = (bf16[384,576]{1,0:T(8,128)(2,1)}, bf16[384,576]{1,0:T(8,128)(2,1)S(1)}, u32[]{:S(2)}) copy-start(bf16[384,576]{1,0:T(8,128)(2,1)S(1)} %fusion.65) | copy-start | bytes 1327108
  110.6 3.0 %copy-start.23 = (f32[768,32]{0,1:T(8,128)S(1)}, f32[768,32]{0,1:T(8,128)}, u32[]{:S(2)}) copy-start(f32[768,32]{0,1:T(8,128)} %get-tuple-element.110) | copy-start | bytes 294916
  113.6 6.2 %copy-start.6 = (f32[384,576]{1,0:T(8,128)S(1)}, f32[384,576]{1,0:T(8,128)}, u32[]{:S(2)}) copy-start(f32[384,576]{1,0:T(8,128)} %copy-done.5) | copy-start | bytes 2654212
  118.6 11.8 %collective-permute-start.2 = (bf16[384,384]{1,0:T(8,128)(2,1)}, bf16[384,384]{1,0:T(8,128)(2,1)}, u32[]{:S(2)}, u32[]{:S(2)}) collective-permute-start(bf16[384,384]{1,0:T(8,128)(2,1)} %fusion.40), channel_id=1, source_target_pairs={{0,1},{1,0},{2,3},{3,2},{4,5},{5,4},{6,7},{7,6},{8,9},{9,8},{10,11... | collective-permute-start | bytes 884744 | tf_op jit(solution)/shard_map/ppermute | solution.py:472
  119.9 3.8 %copy-start.15 = (f32[3,64,3,384]{3,1,2,0:T(8,128)S(1)}, f32[3,64,3,384]{3,1,2,0:T(8,128)}, u32[]{:S(2)}) copy-start(f32[3,64,3,384]{3,1,2,0:T(8,128)} %convolution_multiply_fusion) | copy-start | bytes 2654212
  119.9 3.9 %copy-start.24 = (f32[384,32]{0,1:T(8,128)S(1)}, f32[384,32]{0,1:T(8,128)}, u32[]{:S(2)}) copy-start(f32[384,32]{0,1:T(8,128)} %get-tuple-element.115) | copy-start | bytes 147460
  129.0 2.7 %copy-start.18 = (bf16[384,576]{1,0:T(8,128)(2,1)S(1)}, bf16[384,576]{1,0:T(8,128)(2,1)}, u32[]{:S(2)}) copy-start(bf16[384,576]{1,0:T(8,128)(2,1)} %copy.78) | copy-start | bytes 1327108
  130.3 1.7 copy-start.1
  132.0 1.8 copy-start.17
  135.6 60.1 %copy-start.7 = (f32[384,576]{1,0:T(8,128)S(1)}, f32[384,576]{1,0:T(8,128)}, u32[]{:S(2)}) copy-start(f32[384,576]{1,0:T(8,128)} %copy-done.5) | copy-start | bytes 2654212
  135.6 60.1 %copy-start.9 = (bf16[1,384,576]{2,1,0:T(8,128)(2,1)S(1)}, bf16[1,384,576]{2,1,0:T(8,128)(2,1)}, u32[]{:S(2)}) copy-start(bf16[1,384,576]{2,1,0:T(8,128)(2,1)} %copy-done.8) | copy-start | bytes 1327108
  135.6 60.1 %copy-start.13 = (f32[384,576]{1,0:T(8,128)S(1)}, f32[384,576]{1,0:T(8,128)}, u32[]{:S(2)}) copy-start(f32[384,576]{1,0:T(8,128)} %copy-done.12) | copy-start | bytes 2654212
  135.7 60.1 %copy-start.22 = (f32[384,576]{1,0:T(8,128)S(1)}, f32[384,576]{1,0:T(8,128)}, u32[]{:S(2)}) copy-start(f32[384,576]{1,0:T(8,128)} %get-tuple-element.124) | copy-start | bytes 2654212
  (7 other events, 7.9 us)

commit v4 on v3

--- a/solution.py
+++ b/solution.py
@@ -515,17 +515,16 @@
     query_cosine, query_sine = rope_tables(query_positions)
     k_cos, k_sin = rope_tables(key_positions)
     normed1, inv_rms1, xn = norm_forward(residual, gain_a)
-    key_projection = jnp.dot(xn, qkv_full[:, query_columns:], preferred_element_type=jnp.float32)
-    query_projection = jnp.dot(xn, qkv_full[:, :query_columns], preferred_element_type=jnp.float32)
+    output_projection = jnp.dot(xn, qkv_full, preferred_element_type=jnp.float32)
     query_rows = apply_rotation(
-        query_projection.reshape(row_span, QUERY_HEADS, HEAD_SIZE),
+        output_projection[:, :query_columns].reshape(row_span, QUERY_HEADS, HEAD_SIZE),
         query_cosine,
         query_sine,
         1.0,
     ).astype(jnp.bfloat16)
     keys_local = (
         apply_rotation(
-            key_projection[:, :key_columns].reshape(
+            output_projection[:, query_columns : query_columns + key_columns].reshape(
                 row_span, KEY_VALUE_HEADS, HEAD_SIZE
             ),
             query_cosine,
@@ -535,15 +534,8 @@
         .astype(jnp.bfloat16)
         .reshape(row_span, key_columns)
     )
-    values_local = key_projection[:, key_columns:].astype(jnp.bfloat16)
-    pair_local = jnp.concatenate([keys_local, values_local], axis=1)
-    pair_other = swap_halves(pair_local)
-    d_act = times_transposed(out_cotangent[0], down_full)
-    pair_other, query_rows, d_act = lax.optimization_barrier((pair_other, query_rows, d_act))
-    first = lax.axis_index("cp") == 0
-    every_pair = jnp.concatenate(
-        [jnp.where(first, pair_local, pair_other), jnp.where(first, pair_other, pair_local)], axis=0
-    )
+    values_local = output_projection[:, query_columns + key_columns :].astype(jnp.bfloat16)
+    every_pair = both_halves(jnp.concatenate([keys_local, values_local], axis=1), 0)
     every_key, every_value = every_pair[:, :key_columns], every_pair[:, key_columns:]
     keys_three_axis = every_key.reshape(every_length, KEY_VALUE_HEADS, HEAD_SIZE)
     values_three_axis = every_value.reshape(every_length, KEY_VALUE_HEADS, HEAD_SIZE)
@@ -559,6 +551,7 @@
         jnp.bfloat16
     )
     cotangent = out_cotangent[0]
+    d_act = times_transposed(cotangent, down_full)
     down_grad = transposed_times(act, cotangent)
     d_gate = (d_act * up_val * sigma * (1.0 + gate * (1.0 - sigma))).astype(jnp.bfloat16)
     d_up = (d_act * silu_gate).astype(jnp.bfloat16)

time: 201 us -> 195 us (0.970)
  matrix products: 36.3 us -> 32.4 us
  other arithmetic: 20.1 us -> 17.6 us
    slice x3, local copies, waits for them, and re-layouts: 0.02 us -> 4.81 us  [the longest x1 2.13 us: shards(): output_projection[:, :query_columns]]
    convert_element_type x1 -> x0, other arithmetic: 2.68 us -> none  [shards(): (d_act * up_val * sigma * (1.0 + gate * (1.0 - sigma))).astype(jnp.bfloat16)]
    dot_general x2 -> x0, local copies, waits for them, and re-layouts: 2.39 us -> none  [shards(): jnp.dot(xn, qkv_full[:, :query_columns], preferred_element_type=jnp.float32)]
    dot_general x2 -> x1, matrix products: 4.22 us -> 2.14 us  [shards(): jnp.dot(xn, qkv_full, preferred_element_type=jnp.float32)]
    unnamed x61 -> x65, local copies, waits for them, and re-layouts: 13.1 us -> 12.7 us
  transfers between devices with their start and end apart: 3 -> 3, of which waited for: 1 -> 1; matrix products, arithmetic and copies ran while one was open for 15% -> 12% of each run, Pallas kernels for 24% -> 24%
where the time goes in v4:
time: 195 us; the launch traced here: 194 us
  Pallas kernels  105 us (54%)
  matrix products  32.4 us (17%)
  local copies, waits for them, and re-layouts  25.9 us (13%)
  other arithmetic  17.6 us (9%)
  waiting for transfers between devices  6.02 us (3%)
  starting transfers between devices  5.63 us (3%)
    pallas_call x1, Pallas kernels, reduce_shards(): pl.pallas_call(functools.partial(reduce_kernel, depth, count), out_shape=...  57.9 us
    pallas_call x1, Pallas kernels, gather_shards(): pl.pallas_call(functools.partial(gather_kernel, depth, count), out_shape=...  47.3 us
    unnamed x65, local copies, waits for them, and re-layouts  12.7 us
    dot_general x5, matrix products, times_transposed(): lax.dot_general(left, right, (((1,), (1,)), ((), ())), preferred_element_...  9.66 us
    ppermute x3, waiting for transfers between devices, swap_halves(): return lax.ppermute(value, 'cp', [(0, 1), (1, 0)])  6.02 us
    ppermute x3, starting transfers between devices, swap_halves(): return lax.ppermute(value, 'cp', [(0, 1), (1, 0)])  5.63 us
    another operation x4, other arithmetic  4.23 us
  transfers between devices with their start and end apart: 3, of which 1 were waited for; matrix products, arithmetic and copies ran while one was open for 12% of the time, Pallas kernels for 24%

profile of v4, /device:TPU:0, one launch (start us, length us, event | category | flops | bytes accessed | tf_op | source)
XLA Modules:
  0.0 193.9 jit_solution(8542533029618894720)
XLA Ops:
  0.6 3.0 %collective-permute-start = (s32[1,384]{1,0:T(1,128)}, s32[1,384]{1,0:T(1,128)S(1)}, u32[]{:S(2)}, u32[]{:S(2)}) collective-permute-start(s32[1,384]{1,0:T(1,128)} %param.15), channel_id=1, source_target_pairs={{0,1},{1,0},{2,3},{3,2},{4,5},{5,4},{6,7},{7,6},{8,9},{9,8},{10,11... | collective-permute-start | bytes 4616 | tf_op jit(solution)/shard_map/ppermute | solution.py:472
  10.3 47.3 %shard_map.169 = (bf16[8,72,1536]{2,1,0:T(8,128)(2,1)S(1)}, bf16[8,16,512]{2,1,0:T(8,128)(2,1)S(1)}, bf16[8,72,1536]{2,1,0:T(8,128)(2,1)}, bf16[8,72,1536]{2,1,0:T(8,128)(2,1)}, bf16[8,192,576]{2,1,0:T(8,128)(2,1)}) custom-call(bf16[1,72,1536]{2,1,0:T(8,128)(2,1)S(1)} %maximum_bitcast_fusion.refs_0_, bf16[1,16,512]{2,1,0:T(8,128)(2,1)S(1)} %scatter.9.refs_1_, ...), custom_call_target="tpu_custom_call" | custom-call | tf_op jit(solution)/shard_map/pallas_call | solution.py:146
  58.1 2.1 %fusion.25 = f32[384,960]{0,1:T(8,128)} fusion(bf16[384,576]{1,0:T(8,128)(2,1)S(1)} %fusion.27, bf16[576,1536]{1,0:T(8,128)(2,1)S(1)} %bitcast.128), kind=kOutput, calls=%fused_computation.50 | convolution fusion | flops 424673280 | bytes 3145728 | tf_op jit(solution)/shard_map/dot_general | solution.py:518
  61.3 1.7 slice.121
  63.0 2.1 %slice.127 = f32[384,576]{0,1:T(8,128)} slice(f32[384,960]{0,1:T(8,128)} %fusion.25), slice={[0:384], [0:576]} | slice | bytes 1769472 | tf_op jit(solution)/shard_map/slice | solution.py:520
  68.9 1.4 collective-permute-start.1
  72.3 6.0 %collective-permute-done.1 = bf16[384,384]{0,1:T(8,128)(2,1)S(1)} collective-permute-done((bf16[384,384]{0,1:T(8,128)(2,1)S(1)}, bf16[384,384]{0,1:T(8,128)(2,1)S(1)}, u32[]{:S(2)}, u32[]{:S(2)}) %collective-permute-start.1) | collective-permute-done | bytes 294944 | tf_op jit(solution)/shard_map/ppermute | solution.py:472
  78.5 1.8 fusion.4
  80.2 2.2 %fusion.2 = f32[3,3,384]{2,1,0:T(4,128)S(1)} fusion(f32[3,768,384,3]{2,1,3,0:T(8,128)S(1)} %get-tuple-element.114, f32[3,3,384]{2,1,0:T(4,128)S(1)} %get-tuple-element.113, pred[384,768]{0,1:T(8,128)(4,1)S(1)} %fusion.22), kind=kLoop, calls=%fused_computation.7 | loop fusion | flops 10613376 | bytes 10939392 | tf_op jit(solution)/shard_map/reduce_sum | solution.py:428
  82.4 2.9 %fusion.18 = bf16[3,64,3,384]{3,1,2,0:T(8,128)(2,1)S(1)} fusion(bf16[768,3,64,1]{0,2,3,1:T(8,128)(2,1)S(1)} %bitcast.154, f32[3,768,384,3]{2,1,3,0:T(8,128)S(1)} %get-tuple-element.114, f32[3,3,384]{2,1,0:T(4,128)S(1)} %fusion.2, f32[3,3,384]{2,1,0:T(4,128)S(1)} %get-tuple-element.113, pred[384,768]{0,1:T(8,128)(4,1)S(1)} %fusion.22), kind=kOutput, calls=%fused_computation.41 | convolution fusion | flops 353230848 | bytes 11676672 | tf_op jit(solution)/shard_map/kgnm,mkd->nkgd/dot_general | solution.py:431
  90.2 3.1 %multiply_convert_fusion = (bf16[384,1536]{1,0:T(8,128)(2,1)S(1)}, bf16[384,1536]{1,0:T(8,128)(2,1)S(1)}, bf16[384,1536]{1,0:T(8,128)(2,1)}) fusion(f32[384,1536]{1,0:T(8,128)S(1)} %fusion.60, f32[384,1536]{1,0:T(8,128)S(1)} %fusion.61, bf16[1536,576]{1,0:T(8,128)(2,1)S(1)} %bitcast.159, bf16[1,384,576]{1,2,0:T(8,128)(2,1)S(1)} %copy-done.22), kind=kOutput, calls=%fused_computation.19 | convolution fusion | flops 688324608 | bytes 10469376 | tf_op jit(solution)/shard_map/dot_general | solution.py:386
  94.7 1.8 multiply_reduce_fusion
  97.7 3.6 %fusion.5 = f32[3,64,768,1]{2,1,3,0:T(8,128)} fusion(bf16[384,3,3,64]{0,3,2,1:T(8,128)(2,1)S(1)} %bitcast.152, f32[3,768,384,3]{2,1,3,0:T(8,128)S(1)} %get-tuple-element.114, f32[3,3,384]{2,1,0:T(4,128)S(1)} %log_add_fusion, pred[384,768]{0,1:T(8,128)(4,1)S(1)} %fusion.22), kind=kOutput, calls=%fused_computation.10 | convolution fusion | flops 350355456 | bytes 11957760 | tf_op jit(solution)/shard_map/kgnm,nkgd->mkd/dot_general | solution.py:446
  101.2 3.7 %fusion.1 = bf16[3,3,384,768]{2,3,1,0:T(8,128)(2,1)S(1)} fusion(f32[3,768,384,3]{2,1,3,0:T(8,128)S(1)} %get-tuple-element.114, f32[3,3,384]{2,1,0:T(4,128)S(1)} %bitcast.156, f32[3,3,384]{2,1,0:T(4,128)S(1)} %log_add_fusion, pred[384,768]{0,1:T(8,128)(4,1)S(1)} %fusion.22, bf16[768,3,64,1]{0,2,3,1:T(8,128)(2,1)S(1)} %bitcast.155, ...), kind=kOutput, calls=%fused_computation.2 | convolution fusion | flops 355663872 | bytes 16985088 | tf_op jit(solution)/shard_map/nkgd,mkd->kgnm/dot_general | solution.py:449
  104.9 1.6 fusion.20
  106.6 1.9 convolution_multiply_fusion
  108.5 1.9 fusion.21
  110.7 1.3 copy.78
  115.0 2.0 %copy.84 = bf16[384,576]{1,0:T(8,128)(2,1)} copy(bf16[384,576]{0,1:T(8,128)(2,1)} %bitcast.138) | data formatting | bytes 884736 | tf_op jit(solution)/shard_map/convert_element_type | solution.py:434
  117.0 2.0 %copy.85 = bf16[1,384,576]{1,2,0:T(8,128)(2,1)} copy(bf16[1,384,576]{2,1,0:T(8,128)(2,1)} %fusion.21) | data formatting | bytes 884736
  121.1 1.4 pad_maximum_fusion.refs_7_
  123.7 3.1 %fusion.33 = (bf16[576]{0:T(1024)(128)(2,1)S(1)}, f32[384]{0:T(512)S(1)}, f32[384,576]{1,0:T(8,128)}) fusion(bf16[1,384,576]{2,1,0:T(8,128)(2,1)S(1)} %copy.66, f32[384]{0:T(512)S(1)} %add_rsqrt_fusion.1, f32[576]{0:T(1024)S(1)} %reshape.380, bf16[576,1536]{1,0:T(8,128)(2,1)} %bitcast.131, bf16[384,384]{1,0:T(8,128)(2,1)S(1)} %fusion.41, ...), kind=kOutput, calls=%fused_computation.58 | convolution fusion | flops 427695168 | bytes 3250560 | tf_op jit(solution)/shard_map/dot_general | solution.py:386
  127.1 2.7 %fusion.11.refs_8_ = bf16[768,1536]{1,0:T(8,128)(2,1)} fusion(bf16[384,576]{1,0:T(8,128)(2,1)} %copy-done.15, bf16[384,960]{1,0:T(8,128)(2,1)S(1)} %pad_maximum_fusion.1), kind=kLoop, calls=%fused_computation.18 | loop fusion | flops 9437184 | bytes 3538944 | tf_op jit(solution)/shard_map/concatenate | solution.py:598
  129.9 57.9 %shard_map.170 = (f32[16,512]{1,0:T(8,128)S(1)}, f32[72,1536]{1,0:T(8,128)S(1)}, f32[72,1536]{1,0:T(8,128)S(1)}, f32[192,576]{1,0:T(8,128)S(1)}, f32[72,1536]{1,0:T(8,128)S(1)}) custom-call(bf16[8,16,512]{2,1,0:T(8,128)(2,1)S(1)} %fusion.50.refs_0_, bf16[384,576]{1,0:T(8,128)(2,1)S(1)} %multiply_convert_fusion.3.refs_1_.refs_3_, ...), custom_call_target="tpu_custom_call" | custom-call | tf_op jit(solution)/shard_map/pallas_call | solution.py:349
  (121 shorter events, 34.4 us)
Async XLA Ops:
  0.6 65.8 %collective-permute-start = (s32[1,384]{1,0:T(1,128)}, s32[1,384]{1,0:T(1,128)S(1)}, u32[]{:S(2)}, u32[]{:S(2)}) collective-permute-start(s32[1,384]{1,0:T(1,128)} %param.15), channel_id=1, source_target_pairs={{0,1},{1,0},{2,3},{3,2},{4,5},{5,4},{6,7},{7,6},{8,9},{9,8},{10,11... | collective-permute-start | bytes 4616 | tf_op jit(solution)/shard_map/ppermute | solution.py:472
  4.9 118.8 %copy-start.8 = (bf16[1,384,576]{2,1,0:T(8,128)(2,1)}, bf16[1,384,576]{2,1,0:T(8,128)(2,1)S(1)}, u32[]{:S(2)}) copy-start(bf16[1,384,576]{2,1,0:T(8,128)(2,1)S(1)} %copy.66) | copy-start | bytes 1327108
  57.6 39.2 %copy-start = (bf16[8,72,1536]{2,1,0:T(8,128)(2,1)}, bf16[8,72,1536]{2,1,0:T(8,128)(2,1)S(1)}, u32[]{:S(2)}) copy-start(bf16[8,72,1536]{2,1,0:T(8,128)(2,1)S(1)} %get-tuple-element.44) | copy-start | bytes 5308420
  58.1 7.0 %copy-start.13 = (bf16[384,576]{1,0:T(8,128)(2,1)}, bf16[384,576]{1,0:T(8,128)(2,1)S(1)}, u32[]{:S(2)}) copy-start(bf16[384,576]{1,0:T(8,128)(2,1)S(1)} %fusion.27) | copy-start | bytes 1327108
  60.3 6.2 %copy-start.25 = (s32[1,384]{1,0:T(1,128)S(1)}, s32[1,384]{1,0:T(1,128)}, u32[]{:S(2)}) copy-start(s32[1,384]{1,0:T(1,128)} %param.15) | copy-start | bytes 4612
  68.9 9.3 %collective-permute-start.1 = (bf16[384,384]{0,1:T(8,128)(2,1)S(1)}, bf16[384,384]{0,1:T(8,128)(2,1)S(1)}, u32[]{:S(2)}, u32[]{:S(2)}) collective-permute-start(bf16[384,384]{0,1:T(8,128)(2,1)S(1)} %pad_maximum_fusion.6), channel_id=1, source_target_pairs={{0,1},{1,0},{2,3},{3,2},{4,5},{5,4},{6,7},{7,6},{8,9},{9,8},{10,11... | collective-permute-start | bytes 884744 | tf_op jit(solution)/shard_map/ppermute | solution.py:472
  85.3 12.2 %copy-start.17 = (bf16[3,64,3,384]{3,1,2,0:T(8,128)(2,1)}, bf16[3,64,3,384]{3,1,2,0:T(8,128)(2,1)S(1)}, u32[]{:S(2)}) copy-start(bf16[3,64,3,384]{3,1,2,0:T(8,128)(2,1)S(1)} %fusion.18) | copy-start | bytes 1327108
  85.4 1.6 copy-start.28
  86.5 22.0 %copy-start.4 = (f32[384,576]{1,0:T(8,128)}, f32[384,576]{1,0:T(8,128)S(1)}, u32[]{:S(2)}) copy-start(f32[384,576]{1,0:T(8,128)S(1)} %get-tuple-element.116) | copy-start | bytes 2654212
  87.0 1.5 copy-start.18
  88.5 1.7 copy-start.26
  96.8 4.4 %copy-start.15 = (bf16[384,576]{1,0:T(8,128)(2,1)}, bf16[384,576]{1,0:T(8,128)(2,1)S(1)}, u32[]{:S(2)}) copy-start(bf16[384,576]{1,0:T(8,128)(2,1)S(1)} %fusion.59) | copy-start | bytes 1327108
  106.6 1.9 copy-start.20
  106.6 1.9 copy-start.27
  110.5 3.8 %copy-start.23 = (f32[384,32]{0,1:T(8,128)S(1)}, f32[384,32]{0,1:T(8,128)}, u32[]{:S(2)}) copy-start(f32[384,32]{0,1:T(8,128)} %get-tuple-element.109) | copy-start | bytes 147460
  112.1 6.9 %copy-start.10 = (f32[768,192]{1,0:T(8,128)}, f32[768,192]{1,0:T(8,128)S(1)}, u32[]{:S(2)}) copy-start(f32[768,192]{1,0:T(8,128)S(1)} %copy.78) | copy-start | bytes 1769476
  112.1 2.1 %copy-start.14 = (f32[3,64,3,384]{3,1,2,0:T(8,128)S(1)}, f32[3,64,3,384]{3,1,2,0:T(8,128)}, u32[]{:S(2)}) copy-start(f32[3,64,3,384]{3,1,2,0:T(8,128)} %convolution_multiply_fusion) | copy-start | bytes 2654212
  113.0 9.5 %collective-permute-start.2 = (bf16[384,384]{1,0:T(8,128)(2,1)}, bf16[384,384]{1,0:T(8,128)(2,1)}, u32[]{:S(2)}, u32[]{:S(2)}) collective-permute-start(bf16[384,384]{1,0:T(8,128)(2,1)} %fusion.38), channel_id=1, source_target_pairs={{0,1},{1,0},{2,3},{3,2},{4,5},{5,4},{6,7},{7,6},{8,9},{9,8},{10,11... | collective-permute-start | bytes 884744 | tf_op jit(solution)/shard_map/ppermute | solution.py:472
  114.2 6.8 %copy-start.24 = (bf16[576]{0:T(1024)(128)(2,1)S(1)}, bf16[576]{0:T(1024)(128)(2,1)}, u32[]{:S(2)}) copy-start(bf16[576]{0:T(1024)(128)(2,1)} %get-tuple-element.80) | copy-start | bytes 3460
  121.1 2.6 %copy-start.16 = (bf16[384,576]{1,0:T(8,128)(2,1)S(1)}, bf16[384,576]{1,0:T(8,128)(2,1)}, u32[]{:S(2)}) copy-start(bf16[384,576]{1,0:T(8,128)(2,1)} %copy.79) | copy-start | bytes 1327108
  129.8 59.5 %copy-start.5 = (f32[384,576]{1,0:T(8,128)S(1)}, f32[384,576]{1,0:T(8,128)}, u32[]{:S(2)}) copy-start(f32[384,576]{1,0:T(8,128)} %copy-done.4) | copy-start | bytes 2654212
  129.8 59.5 %copy-start.7 = (f32[384,576]{1,0:T(8,128)S(1)}, f32[384,576]{1,0:T(8,128)}, u32[]{:S(2)}) copy-start(f32[384,576]{1,0:T(8,128)} %copy-done.6) | copy-start | bytes 2654212
  129.8 59.5 %copy-start.9 = (bf16[1,384,576]{2,1,0:T(8,128)(2,1)S(1)}, bf16[1,384,576]{2,1,0:T(8,128)(2,1)}, u32[]{:S(2)}) copy-start(bf16[1,384,576]{2,1,0:T(8,128)(2,1)} %copy-done.8) | copy-start | bytes 1327108
  129.9 59.5 %copy-start.21 = (f32[384,576]{1,0:T(8,128)S(1)}, f32[384,576]{1,0:T(8,128)}, u32[]{:S(2)}) copy-start(f32[384,576]{1,0:T(8,128)} %get-tuple-element.118) | copy-start | bytes 2654212
  (8 other events, 8.9 us)
